TPU v7x, 32 devices: a whole 2x2x4 slice. The times are simulated.
32 devices in a mesh: dp: 8 (over y, x, core), sp: 4 (over z).
Axes of the slice: x: 2, y: 2, z: 4, core: 2. Of those that a mesh axis runs over, the one named last changes fastest.
Arguments:
- layer_input: bfloat16 [8, 512, 2048], P('dp', 'sp'), may hold values from -6 to 6
- lengths: int32 [8], P('dp'), may hold values from 128 to 512, as said below
- cotangent: bfloat16 [8, 512, 2048], P('dp', 'sp'), may hold values from -6 to 6
- ln1_gain: bfloat16 [2048], P(('dp', 'sp')), may hold values from 0.5 to 1.5
- ln1_bias: bfloat16 [2048], P(('dp', 'sp')), may hold values from -3 to 3
- ln2_gain: bfloat16 [2048], P(('dp', 'sp')), may hold values from 0.5 to 1.5
- ln2_bias: bfloat16 [2048], P(('dp', 'sp')), may hold values from -3 to 3
- qkv_weight: bfloat16 [2048, 6144], P('dp', 'sp'), may hold values from -0.125 to 0.125
- qkv_bias: bfloat16 [6144], P(('dp', 'sp')), may hold values from -3 to 3
- out_weight: bfloat16 [2048, 2048], P('sp', 'dp'), may hold values from -1 to 1
- gate_weight: bfloat16 [2048, 5632], P('dp', 'sp'), may hold values from -0.125 to 0.125
- up_weight: bfloat16 [2048, 5632], P('dp', 'sp'), may hold values from -0.125 to 0.125
- down_weight: bfloat16 [2048, 5632], P('dp', 'sp'), may hold values from -0.078125 to 0.078125
Outputs:
- layer_output: bfloat16 [8, 512, 2048], P('dp', 'sp')
- input_grad: float32 [8, 512, 2048], P('dp', 'sp')
- ln1_gain_grad: float32 [2048], P(('dp', 'sp'))
- ln1_bias_grad: float32 [2048], P(('dp', 'sp'))
- ln2_gain_grad: float32 [2048], P(('dp', 'sp'))
- ln2_bias_grad: float32 [2048], P(('dp', 'sp'))
- qkv_weight_grad: float32 [2048, 6144], P('dp', 'sp')
- qkv_bias_grad: float32 [6144], P(('dp', 'sp'))
- out_weight_grad: float32 [2048, 2048], P('sp', 'dp')
- gate_weight_grad: float32 [2048, 5632], P('dp', 'sp')
- up_weight_grad: float32 [2048, 5632], P('dp', 'sp')
- down_weight_grad: float32 [2048, 5632], P('dp', 'sp')
Inputs may be any that keep to these rules, and one draw needn't show every extreme that they name: Row r holds one sequence in its first lengths[r] slots; some row is full in every draw.
All inputs are finite; a program needn't handle non-finite values.
Results may differ from a plain program's by a relative error of at most 0.015.
Values may be sent and summed in bfloat16 or wider, within the bound.
A program may use at most 192 MiB of HBM per device.

v0:
```python
import jax
import jax.numpy as jnp
from jax import lax
from jax.sharding import PartitionSpec as P

HEAD_DIM = 64
ROT = 16


eps_norm = 1e-05
theta = 10000.0
neg_large = -1e30


def norm_forward(hidden, gain, bias):
    centre = hidden - jnp.mean(hidden, axis=-1, keepdims=True)
    rstd = lax.rsqrt(jnp.mean(centre * centre, axis=-1, keepdims=True) + eps_norm)
    normed = centre * rstd
    return (normed * gain + bias, normed, rstd)


def norm_backward(grad, normed, rstd, gain):
    gain_grad = jnp.sum(grad * normed, axis=0)
    bias_grad = jnp.sum(grad, axis=0)
    scaled = grad * gain
    input_part = rstd * (
        scaled
        - jnp.mean(scaled, axis=-1, keepdims=True)
        - normed * jnp.mean(scaled * normed, axis=-1, keepdims=True)
    )
    return (input_part, gain_grad, bias_grad)


def rotate(tensor, cosine, sine, direction):
    half_rot = ROT // 2
    first = tensor[..., :half_rot]
    second = tensor[..., half_rot:ROT]
    cos_part = cosine[None, :, None, :]
    sin_part = sine[None, :, None, :] * direction
    return jnp.concatenate(
        [
            first * cos_part - second * sin_part,
            second * cos_part + first * sin_part,
            tensor[..., ROT:],
        ],
        axis=-1,
    )


def rotary_tables(position_list):
    freq = theta ** (-(jnp.arange(ROT // 2, dtype=jnp.float32) * 2.0) / ROT)
    angles = position_list.astype(jnp.float32)[:, None] * freq[None, :]
    return (jnp.cos(angles), jnp.sin(angles))


def contract_rows(left, right):
    return lax.dot_general(
        left, right, (((0,), (0,)), ((), ())), preferred_element_type=jnp.float32
    )


def contract_cols(left, right):
    return lax.dot_general(
        left, right, (((1,), (1,)), ((), ())), preferred_element_type=jnp.float32
    )


def block_scores(query_block, keys, first_row, length, block_rows):
    softmax_scale = HEAD_DIM ** (-0.5)
    key_pos = jnp.arange(keys.shape[0], dtype=jnp.int32)
    query_pos = first_row + jnp.arange(block_rows, dtype=jnp.int32)
    scores = (
        jnp.einsum("qhd,khd->hqk", query_block, keys, preferred_element_type=jnp.float32)
        * softmax_scale
    )
    allowed = (key_pos[None, :] <= query_pos[:, None]) & (key_pos < length)[None, :]
    return jnp.where(allowed[None], scores, neg_large)


def attend_forward(queries, keys, values, length, block_rows):

    def one_block(block_index):
        first_row = block_index * block_rows
        query_block = lax.dynamic_slice_in_dim(queries, first_row, block_rows, 0)
        scores = block_scores(query_block, keys, first_row, length, block_rows)
        top_score = jnp.max(scores, axis=-1, keepdims=True)
        total = jnp.sum(jnp.exp(scores - top_score), axis=-1, keepdims=True)
        log_total = top_score + jnp.log(total)
        attn_weights = jnp.exp(scores - log_total).astype(jnp.bfloat16)
        result = jnp.einsum(
            "hqk,khd->qhd", attn_weights, values, preferred_element_type=jnp.float32
        )
        return (result.astype(jnp.bfloat16), log_total[..., 0])

    results, log_totals = lax.map(
        one_block, jnp.arange(queries.shape[0] // block_rows, dtype=jnp.int32)
    )
    return (results.reshape(queries.shape), log_totals)


def attend_backward(queries, keys, values, grad_out, log_totals, length, block_rows):
    softmax_scale = HEAD_DIM ** (-0.5)

    def one_block(carry, block_index):
        key_grad, value_grad = carry
        first_row = block_index * block_rows
        query_block = lax.dynamic_slice_in_dim(queries, first_row, block_rows, 0)
        grad_block = lax.dynamic_slice_in_dim(grad_out, first_row, block_rows, 0)
        scores = block_scores(query_block, keys, first_row, length, block_rows)
        weights_full = jnp.exp(scores - log_totals[block_index][..., None])
        attn_weights = weights_full.astype(jnp.bfloat16)
        weight_grad = jnp.einsum(
            "qhd,khd->hqk", grad_block, values, preferred_element_type=jnp.float32
        )
        delta = jnp.sum(weight_grad * weights_full, axis=-1, keepdims=True)
        score_grad = (weights_full * (weight_grad - delta)).astype(jnp.bfloat16)
        query_grad = (
            jnp.einsum("hqk,khd->qhd", score_grad, keys, preferred_element_type=jnp.float32)
            * softmax_scale
        )
        key_grad = (
            key_grad
            + jnp.einsum(
                "hqk,qhd->khd", score_grad, query_block, preferred_element_type=jnp.float32
            )
            * softmax_scale
        )
        value_grad = value_grad + jnp.einsum(
            "hqk,qhd->khd", attn_weights, grad_block, preferred_element_type=jnp.float32
        )
        return ((key_grad, value_grad), query_grad)

    zeros = jnp.zeros(keys.shape, jnp.float32)
    (key_grad, value_grad), query_grad = lax.scan(
        one_block, (zeros, zeros), jnp.arange(queries.shape[0] // block_rows, dtype=jnp.int32)
    )
    return (query_grad.reshape(queries.shape), key_grad, value_grad)


def feed_forward(tokens, grads_out, w_gate, w_up, w_down):
    gate = jnp.dot(tokens, w_gate, preferred_element_type=jnp.float32)
    up_proj = jnp.dot(tokens, w_up, preferred_element_type=jnp.float32)
    sigmoid_gate = jax.nn.sigmoid(gate)
    silu_gate = gate * sigmoid_gate
    hidden_act = (silu_gate * up_proj).astype(jnp.bfloat16)
    mixed = contract_cols(hidden_act, w_down)
    act_grad = jnp.dot(grads_out, w_down, preferred_element_type=jnp.float32)
    up_grad = (act_grad * silu_gate).astype(jnp.bfloat16)
    gate_grad = (act_grad * up_proj * sigmoid_gate * (1.0 + gate * (1.0 - sigmoid_gate))).astype(
        jnp.bfloat16
    )
    token_grad = contract_cols(gate_grad, w_gate) + contract_cols(up_grad, w_up)
    weight_grads = (
        contract_rows(tokens, gate_grad),
        contract_rows(tokens, up_grad),
        contract_rows(grads_out, hidden_act),
    )
    return (mixed, token_grad, weight_grads)


def per_device(
    layer_input,
    lengths,
    cotangent,
    ln1_gain,
    ln1_bias,
    ln2_gain,
    ln2_bias,
    qkv_weight,
    qkv_bias,
    out_weight,
    gate_weight,
    up_weight,
    down_weight,
):
    row_count, slot_count, width = layer_input.shape
    sp_count = lax.axis_size("sp")
    sp_index = lax.axis_index("sp")
    tokens_dev = row_count * slot_count
    seq_len = slot_count * sp_count
    block_rows = min(512, seq_len)
    local_width = width // sp_count
    local_heads = local_width // HEAD_DIM
    local_cols = 3 * local_width
    positions = sp_index * slot_count + jnp.arange(slot_count, dtype=jnp.int32)
    valid = (positions[None, :] < lengths[:, None]).astype(jnp.float32).reshape(tokens_dev, 1)
    small = (
        lax.all_gather(ln1_gain, ("dp", "sp"), axis=0, tiled=True),
        lax.all_gather(ln1_bias, ("dp", "sp"), axis=0, tiled=True),
        lax.all_gather(ln2_gain, ("dp", "sp"), axis=0, tiled=True),
        lax.all_gather(ln2_bias, ("dp", "sp"), axis=0, tiled=True),
        lax.all_gather(qkv_bias, ("dp", "sp"), axis=0, tiled=True),
    )
    gain_one = small[0].astype(jnp.float32)
    bias_one = small[1].astype(jnp.float32)
    gain_two = small[2].astype(jnp.float32)
    bias_two = small[3].astype(jnp.float32)
    b_qkv = small[4].astype(jnp.float32)
    qkv_cols, out_rows, gate_cols, up_cols, down_cols = (
        lax.all_gather(qkv_weight, "dp", axis=0, tiled=True),
        lax.all_gather(out_weight, "dp", axis=1, tiled=True),
        lax.all_gather(gate_weight, "dp", axis=0, tiled=True),
        lax.all_gather(up_weight, "dp", axis=0, tiled=True),
        lax.all_gather(down_weight, "dp", axis=0, tiled=True),
    )
    w_gate, w_up, w_down = (gate_cols, up_cols, down_cols)
    hidden_in = layer_input.astype(jnp.float32).reshape(tokens_dev, width)
    normed_one, unit_one, rstd_one = norm_forward(hidden_in, gain_one, bias_one)
    normed_one = normed_one.astype(jnp.bfloat16)
    cosine, sine = rotary_tables(jnp.arange(seq_len, dtype=jnp.int32))
    row_normed = lax.all_gather(
        normed_one.reshape(row_count, slot_count, width), "sp", axis=1, tiled=True
    ).reshape(row_count * seq_len, width)
    bias_local = lax.dynamic_slice_in_dim(b_qkv, sp_index * local_cols, local_cols)
    qkv_raw = (
        jnp.dot(row_normed, qkv_cols, preferred_element_type=jnp.float32) + bias_local
    ).reshape(row_count, seq_len, local_heads, 3, HEAD_DIM)
    query_heads = (
        rotate(qkv_raw[:, :, :, 0], cosine, sine, 1.0)
        .astype(jnp.bfloat16)
        .reshape(row_count, seq_len, local_width)
    )
    key_heads = (
        rotate(qkv_raw[:, :, :, 1], cosine, sine, 1.0)
        .astype(jnp.bfloat16)
        .reshape(row_count, seq_len, local_width)
    )
    value_heads = qkv_raw[:, :, :, 2].astype(jnp.bfloat16).reshape(row_count, seq_len, local_width)
    head_shape = (seq_len, local_heads, HEAD_DIM)

    def forward_row(row_data):
        row_query, row_key, row_value, row_length = row_data
        return attend_forward(
            row_query.reshape(head_shape),
            row_key.reshape(head_shape),
            row_value.reshape(head_shape),
            row_length,
            block_rows,
        )

    attended_heads, log_totals = lax.map(
        forward_row, (query_heads, key_heads, value_heads, lengths)
    )
    attended_heads = attended_heads.reshape(row_count, seq_len, local_width)
    attended_flat = attended_heads.reshape(row_count * seq_len, local_width)
    branch_part = jnp.dot(attended_flat, out_rows, preferred_element_type=jnp.float32).reshape(
        row_count, seq_len, width
    )
    branch = lax.psum_scatter(branch_part, "sp", scatter_dimension=1, tiled=True).reshape(
        tokens_dev, width
    )
    resid = hidden_in + branch
    normed_two, unit_two, rstd_two = norm_forward(resid, gain_two, bias_two)
    normed_two = normed_two.astype(jnp.bfloat16)
    out_grad = (cotangent.astype(jnp.float32).reshape(tokens_dev, width) * valid).astype(
        jnp.bfloat16
    )
    row_tokens, row_grads = (
        lax.all_gather(normed_two.reshape(row_count, slot_count, width), "sp", axis=1, tiled=True),
        lax.all_gather(out_grad.reshape(row_count, slot_count, width), "sp", axis=1, tiled=True),
    )
    mixed_part, token_grad_part, mlp_grads = feed_forward(
        row_tokens.reshape(row_count * seq_len, width),
        row_grads.reshape(row_count * seq_len, width),
        w_gate,
        w_up,
        w_down,
    )
    mixed, normed_two_grad = (
        lax.psum_scatter(
            mixed_part.reshape(row_count, seq_len, width), "sp", scatter_dimension=1, tiled=True
        ),
        lax.psum_scatter(
            token_grad_part.reshape(row_count, seq_len, width),
            "sp",
            scatter_dimension=1,
            tiled=True,
        ),
    )
    mixed = mixed.reshape(tokens_dev, width)
    normed_two_grad = normed_two_grad.reshape(tokens_dev, width)
    layer_output = (
        (valid * (resid + mixed)).astype(jnp.bfloat16).reshape(row_count, slot_count, width)
    )
    resid_part, gain_two_grad, bias_two_grad = norm_backward(
        normed_two_grad, unit_two, rstd_two, gain_two
    )
    resid_grad = out_grad.astype(jnp.float32) + resid_part
    branch_grad = resid_grad.astype(jnp.bfloat16)
    row_branch = lax.all_gather(
        branch_grad.reshape(row_count, slot_count, width), "sp", axis=1, tiled=True
    ).reshape(row_count * seq_len, width)
    out_weight_grad = contract_rows(attended_flat, row_branch)
    attended_grad_heads = (
        contract_cols(row_branch, out_rows)
        .astype(jnp.bfloat16)
        .reshape(row_count, seq_len, local_width)
    )

    def backward_row(row_data):
        row_query, row_key, row_value, row_grad, row_totals, row_length = row_data
        query_grad, key_grad, value_grad = attend_backward(
            row_query.reshape(head_shape),
            row_key.reshape(head_shape),
            row_value.reshape(head_shape),
            row_grad.reshape(head_shape),
            row_totals,
            row_length,
            block_rows,
        )
        return (
            query_grad.astype(jnp.bfloat16).reshape(seq_len, local_width),
            key_grad.astype(jnp.bfloat16).reshape(seq_len, local_width),
            value_grad.astype(jnp.bfloat16).reshape(seq_len, local_width),
        )

    query_grads, key_grads, value_grads = lax.map(
        backward_row,
        (query_heads, key_heads, value_heads, attended_grad_heads, log_totals, lengths),
    )
    row_shape = (row_count, seq_len, local_heads, HEAD_DIM)
    query_raw = rotate(query_grads.astype(jnp.float32).reshape(row_shape), cosine, sine, -1.0)
    key_raw = rotate(key_grads.astype(jnp.float32).reshape(row_shape), cosine, sine, -1.0)
    value_raw = value_grads.astype(jnp.float32).reshape(row_shape)
    qkv_grad = (
        jnp.stack([query_raw, key_raw, value_raw], axis=3)
        .reshape(row_count * seq_len, local_cols)
        .astype(jnp.bfloat16)
    )
    bias_local_grad = jnp.sum(qkv_grad.astype(jnp.float32), axis=0)
    qkv_bias_full = lax.dynamic_update_slice(
        jnp.zeros((3 * width,), jnp.float32), bias_local_grad, (sp_index * local_cols,)
    )
    qkv_weight_grad = contract_rows(row_normed, qkv_grad)
    normed_part = contract_cols(qkv_grad, qkv_cols).reshape(row_count, seq_len, width)
    normed_one_grad = (
        lax.psum_scatter(normed_part.astype(jnp.bfloat16), "sp", scatter_dimension=1, tiled=True)
        .astype(jnp.float32)
        .reshape(tokens_dev, width)
    )
    input_part, gain_one_grad, bias_one_grad = norm_backward(
        normed_one_grad, unit_one, rstd_one, gain_one
    )
    input_grad = (resid_grad + input_part).reshape(row_count, slot_count, width)
    small_sums = (
        lax.psum_scatter(gain_one_grad, ("dp", "sp"), scatter_dimension=0, tiled=True),
        lax.psum_scatter(bias_one_grad, ("dp", "sp"), scatter_dimension=0, tiled=True),
        lax.psum_scatter(gain_two_grad, ("dp", "sp"), scatter_dimension=0, tiled=True),
        lax.psum_scatter(bias_two_grad, ("dp", "sp"), scatter_dimension=0, tiled=True),
        lax.psum_scatter(qkv_bias_full, ("dp", "sp"), scatter_dimension=0, tiled=True),
    )
    row_sums = (
        lax.psum_scatter(
            qkv_weight_grad.astype(jnp.bfloat16), "dp", scatter_dimension=0, tiled=True
        ).astype(jnp.float32),
        lax.psum_scatter(
            out_weight_grad.astype(jnp.bfloat16), "dp", scatter_dimension=1, tiled=True
        ).astype(jnp.float32),
        lax.psum_scatter(
            mlp_grads[0].astype(jnp.bfloat16), "dp", scatter_dimension=0, tiled=True
        ).astype(jnp.float32),
        lax.psum_scatter(
            mlp_grads[1].astype(jnp.bfloat16), "dp", scatter_dimension=0, tiled=True
        ).astype(jnp.float32),
        lax.psum_scatter(
            mlp_grads[2].astype(jnp.bfloat16), "dp", scatter_dimension=0, tiled=True
        ).astype(jnp.float32),
    )
    return (
        layer_output,
        input_grad,
        small_sums[0],
        small_sums[1],
        small_sums[2],
        small_sums[3],
        row_sums[0],
        small_sums[4],
        row_sums[1],
        row_sums[2],
        row_sums[3],
        row_sums[4],
    )


def solution(mesh):
    placed = (
        P("dp", "sp", None),
        P("dp"),
        P("dp", "sp", None),
        P(("dp", "sp")),
        P(("dp", "sp")),
        P(("dp", "sp")),
        P(("dp", "sp")),
        P("dp", "sp"),
        P(("dp", "sp")),
        P("sp", "dp"),
        P("dp", "sp"),
        P("dp", "sp"),
        P("dp", "sp"),
    )
    return jax.shard_map(
        per_device,
        mesh=mesh,
        in_specs=placed,
        out_specs=(
            P("dp", "sp", None),
            P("dp", "sp", None),
            P(("dp", "sp")),
            P(("dp", "sp")),
            P(("dp", "sp")),
            P(("dp", "sp")),
            P("dp", "sp"),
            P(("dp", "sp")),
            P("sp", "dp"),
            P("dp", "sp"),
            P("dp", "sp"),
            P("dp", "sp"),
        ),
        check_vma=False,
    )
```

profile of v0, /device:TPU:0, one launch (start us, length us, event | category | flops | bytes accessed | tf_op | source)
XLA Modules:
  0.0 1073.6 jit_solution(3147372473972999172)
XLA Ops:
  11.5 42.4 %all-reduce.11 = (bf16[2048]{0:T(1024)(128)(2,1)S(1)}, bf16[2048]{0:T(1024)(128)(2,1)S(1)}, bf16[2048]{0:T(1024)(128)(2,1)S(1)}, bf16[2048]{0:T(1024)(128)(2,1)S(1)}, bf16[6144]{0:T(1024)(128)(2,1)S(1)}) all-reduce(bf16[2048]{0:T(1024)(128)(2,1)S(1)} %dynamic-update-slice.4, ...), channel_id=1, replica_groups=mesh['dp'=8,'sp'=4] {'dp','sp'}, use_global_device_ids=true, to_apply=%add.4 | all-reduce | flops 14336 | bytes 57344
  53.9 1.2 convert_reduce_fusion.1
  55.2 1.3 fusion.38
  56.5 2.2 fusion.48
  62.5 42.2 %all-gather.10.cloned.1.call-done = bf16[1,512,2048]{2,1,0:T(8,128)(2,1)} async-done(((bf16[1,128,2048]{2,1,0:T(8,128)(2,1)}), bf16[1,512,2048]{2,1,0:T(8,128)(2,1)}) %all-gather.10.cloned.1.call-update) | async-done | bytes 2097168 | tf_op jit(solution)/shard_map/all_gather | solution.py:211
  104.7 46.2 %all-gather.12.cloned.1.call-done = bf16[2048,1536]{1,0:T(8,128)(2,1)} async-done(((bf16[256,1536]{1,0:T(8,128)(2,1)}), bf16[2048,1536]{1,0:T(8,128)(2,1)}) %all-gather.12.cloned.1.call-update) | async-done | bytes 6291472 | tf_op jit(solution)/shard_map/all_gather | solution.py:200
  150.8 8.5 convolution_add_fusion
  159.3 3.6 copy.41
  163.0 1.8 fusion.70
  165.2 1.5 fusion
  166.8 1.7 exponential_reduce_fusion
  168.5 1.5 copy-done
  170.0 3.5 convolution_convert_fusion.7
  173.5 7.4 all-gather.14.cloned.1.call-done
  181.0 4.9 convolution_bitcast_fusion.1
  186.6 76.2 %reduce-scatter.10.cloned.1.call-done = f32[1,128,2048]{2,1,0:T(8,128)} async-done(((f32[1,512,2048]{2,1,0:T(8,128)}), f32[1,128,2048]{2,1,0:T(8,128)}) %reduce-scatter.10.cloned.1.call-update) | async-done | bytes 1048592 | tf_op jit(solution)/shard_map/reduce_scatter | solution.py:249
  262.8 1.5 fusion.59
  264.4 1.5 multiply_reduce_fusion.2
  265.9 1.1 add_convert_fusion
  267.8 0.9 multiply_convert_fusion.4
  269.7 38.8 %all-gather.20.cloned.1.call-done = bf16[2048,1408]{1,0:T(8,128)(2,1)} async-done(((bf16[256,1408]{1,0:T(8,128)(2,1)}), bf16[2048,1408]{1,0:T(8,128)(2,1)}) %all-gather.20.cloned.1.call-update) | async-done | bytes 5767184 | tf_op jit(solution)/shard_map/all_gather | solution.py:203
  308.6 48.1 %all-gather.16.cloned.1.call-done = bf16[1,512,2048]{2,1,0:T(8,128)(2,1)} async-done(((bf16[1,128,2048]{2,1,0:T(8,128)(2,1)}), bf16[1,512,2048]{2,1,0:T(8,128)(2,1)}) %all-gather.16.cloned.1.call-update) | async-done | bytes 2097168 | tf_op jit(solution)/shard_map/all_gather | solution.py:259
  356.6 8.2 fusion.12
  364.9 35.9 %all-gather.18.cloned.1.call-done = bf16[2048,1408]{1,0:T(8,128)(2,1)} async-done(((bf16[256,1408]{1,0:T(8,128)(2,1)}), bf16[2048,1408]{1,0:T(8,128)(2,1)}) %all-gather.18.cloned.1.call-update) | async-done | bytes 5767184 | tf_op jit(solution)/shard_map/all_gather | solution.py:202
  400.7 8.3 fusion.14
  409.0 39.9 %all-gather.24.cloned.1.call-done = bf16[1,512,2048]{2,1,0:T(8,128)(2,1)} async-done(((bf16[1,128,2048]{2,1,0:T(8,128)(2,1)}), bf16[1,512,2048]{2,1,0:T(8,128)(2,1)}) %all-gather.24.cloned.1.call-update) | async-done | bytes 2097168 | tf_op jit(solution)/shard_map/all_gather | solution.py:260
  448.9 44.1 %all-gather.22.cloned.1.call-done = bf16[2048,1408]{1,0:T(8,128)(2,1)} async-done(((bf16[256,1408]{1,0:T(8,128)(2,1)}), bf16[2048,1408]{1,0:T(8,128)(2,1)}) %all-gather.22.cloned.1.call-update) | async-done | bytes 5767184 | tf_op jit(solution)/shard_map/all_gather | solution.py:204
  493.0 10.4 multiply_convert_fusion.1
  503.5 3.4 fusion.71
  507.0 7.7 add_bitcast_fusion
  514.9 8.5 convolution_bitcast_fusion
  523.5 68.0 %reduce-scatter.14.cloned.1.call-done = f32[1,128,2048]{2,1,0:T(8,128)} async-done(((f32[1,512,2048]{2,1,0:T(8,128)}), f32[1,128,2048]{2,1,0:T(8,128)}) %reduce-scatter.14.cloned.1.call-update) | async-done | bytes 1048592 | tf_op jit(solution)/shard_map/reduce_scatter | solution.py:273
  591.6 2.4 fusion.49
  595.0 76.3 %reduce-scatter.12.cloned.1.call-done = f32[1,128,2048]{2,1,0:T(8,128)} async-done(((f32[1,512,2048]{2,1,0:T(8,128)}), f32[1,128,2048]{2,1,0:T(8,128)}) %reduce-scatter.12.cloned.1.call-update) | async-done | bytes 1048592 | tf_op jit(solution)/shard_map/reduce_scatter | solution.py:270
  671.2 4.0 fusion.69
  675.3 7.9 convolution_convert_fusion.2
  683.3 1.3 copy-done.33
  684.6 7.5 convolution_convert_fusion.1
  692.6 0.9 copy-done.34
  693.5 7.5 convolution_convert_fusion
  701.1 20.7 %all-gather.26.cloned.1.call-done = bf16[1,512,2048]{2,1,0:T(8,128)(2,1)} async-done(((bf16[1,128,2048]{2,1,0:T(8,128)(2,1)}), bf16[1,512,2048]{2,1,0:T(8,128)(2,1)}) %all-gather.26.cloned.1.call-update) | async-done | bytes 2097168 | tf_op jit(solution)/shard_map/all_gather | solution.py:290
  721.8 4.2 convolution_convert_fusion.4
  726.0 3.5 fusion.22
  729.5 7.9 multiply_reduce_fusion
  737.7 7.3 multiply_convert_fusion
  746.0 1.4 fusion.32
  747.7 2.0 slice-done.1
  749.7 2.3 fusion.26
  752.5 4.8 fusion.3
  757.3 7.0 convolution_convert_fusion.3
  764.4 19.0 %reduce-scatter.22.cloned.1.call-done = bf16[256,1408]{1,0:T(8,128)(2,1)} async-done(((bf16[2048,1408]{1,0:T(8,128)(2,1)}), bf16[256,1408]{1,0:T(8,128)(2,1)}) %reduce-scatter.22.cloned.1.call-update) | async-done | bytes 720912 | tf_op jit(solution)/shard_map/reduce_scatter | solution.py:359
  783.4 2.3 convert_element_type.316
  785.7 60.1 %reduce-scatter.24.cloned.1.call-done = bf16[256,1408]{1,0:T(8,128)(2,1)} async-done(((bf16[2048,1408]{1,0:T(8,128)(2,1)}), bf16[256,1408]{1,0:T(8,128)(2,1)}) %reduce-scatter.24.cloned.1.call-update) | async-done | bytes 720912 | tf_op jit(solution)/shard_map/reduce_scatter | solution.py:362
  845.8 2.3 convert_element_type.318
  848.1 60.4 %reduce-scatter.26.cloned.1.call-done = bf16[256,1408]{1,0:T(8,128)(2,1)} async-done(((bf16[2048,1408]{1,0:T(8,128)(2,1)}), bf16[256,1408]{1,0:T(8,128)(2,1)}) %reduce-scatter.26.cloned.1.call-update) | async-done | bytes 720912 | tf_op jit(solution)/shard_map/reduce_scatter | solution.py:365
  908.6 2.3 convert_element_type.320
  911.2 41.7 %reduce-scatter.20.cloned.1.call-done = bf16[512,256]{1,0:T(8,128)(2,1)} async-done(((bf16[512,2048]{1,0:T(8,128)(2,1)}), bf16[512,256]{1,0:T(8,128)(2,1)}) %reduce-scatter.20.cloned.1.call-update) | async-done | bytes 262160 | tf_op jit(solution)/shard_map/reduce_scatter | solution.py:356
  952.9 1.8 convert_element_type.314
  954.7 44.4 %reduce-scatter.16.cloned.1.call-done = bf16[1,128,2048]{2,1,0:T(8,128)(2,1)} async-done(((bf16[1,512,2048]{2,1,0:T(8,128)(2,1)}), bf16[1,128,2048]{2,1,0:T(8,128)(2,1)}) %reduce-scatter.16.cloned.1.call-update) | async-done | bytes 524304 | tf_op jit(solution)/shard_map/reduce_scatter | solution.py:337
  999.1 1.5 fusion.39
  1000.6 2.5 convert_reduce_fusion.2
  1003.2 40.5 %all-reduce.10 = (f32[2048]{0:T(1024)S(1)}, f32[2048]{0:T(1024)S(1)}, f32[2048]{0:T(1024)S(1)}, f32[2048]{0:T(1024)S(1)}, f32[6144]{0:T(1024)S(1)}) all-reduce(f32[2048]{0:T(1024)S(1)} %get-tuple-element.124, f32[2048]{0:T(1024)S(1)} %get-tuple-element.166, ...), channel_id=6, replica_groups=mesh['dp'=8,'sp'=4] {'dp','sp'}, use_global_device_ids=true, to_apply=%region_16.17.clone | all-reduce | flops 14336 | bytes 114688
  1046.7 17.4 %reduce-scatter.18.cloned.1.call-done = bf16[256,1536]{1,0:T(8,128)(2,1)} async-done(((bf16[2048,1536]{1,0:T(8,128)(2,1)}), bf16[256,1536]{1,0:T(8,128)(2,1)}) %reduce-scatter.18.cloned.1.call-update) | async-done | bytes 786448 | tf_op jit(solution)/shard_map/reduce_scatter | solution.py:353
  1064.1 2.5 convert_element_type.311
  (165 shorter events, 17.5 us)
Async XLA Ops:
  7.2 97.5 %all-gather.10.cloned.1.call-start = ((), (), s32[]{:S(2)}) async-start(), calls=%async_computation.9 | async-start | bytes 2621440 | tf_op jit(solution)/shard_map/all_gather | solution.py:211
  53.9 105.4 %copy-start.18 = (f32[2048]{0:T(1024)}, f32[2048]{0:T(1024)S(1)}, u32[]{:S(2)}) copy-start(f32[2048]{0:T(1024)S(1)} %convert_element_type.271) | copy-start | bytes 24580
  55.1 6.5 copy-start.24
  56.5 5.1 copy-start.27
  58.8 92.1 %all-gather.12.cloned.1.call-start = ((), (), s32[]{:S(2)}) async-start(), calls=%async_computation.10 | async-start | bytes 7077888 | tf_op jit(solution)/shard_map/all_gather | solution.py:200
  59.5 121.4 %all-gather.14.cloned.1.call-start = ((), (), s32[]{:S(2)}) async-start(), calls=%async_computation.11 | async-start | bytes 2359296 | tf_op jit(solution)/shard_map/all_gather | solution.py:201
  60.3 202.6 %reduce-scatter.10.cloned.1.call-start = ((), (), s32[]{:S(2)}) async-start(), calls=%async_computation.12 | async-start | bytes 5242880 | tf_op jit(solution)/shard_map/reduce_scatter | solution.py:249
  165.0 1.7 copy-start.12
  165.0 1.7 copy-start.14
  165.1 1.6 copy-start.6
  165.2 1.6 copy-start.8
  166.7 3.3 copy-start
  170.0 3.5 copy-start.16
  173.5 7.4 copy-start.10
  185.9 77.0 %copy-start.1 = (bf16[1,128,2048]{2,1,0:T(8,128)(2,1)S(1)}, bf16[1,128,2048]{2,1,0:T(8,128)(2,1)}, u32[]{:S(2)}) copy-start(bf16[1,128,2048]{2,1,0:T(8,128)(2,1)} %param.13) | copy-start | bytes 1572868
  185.9 122.7 %all-gather.20.cloned.1.call-start = ((), (), s32[]{:S(2)}) async-start(), calls=%async_computation.15 | async-start | bytes 6488064 | tf_op jit(solution)/shard_map/all_gather | solution.py:203
  186.5 170.1 %all-gather.16.cloned.1.call-start = ((), (), s32[]{:S(2)}) async-start(), calls=%async_computation.13 | async-start | bytes 2621440 | tf_op jit(solution)/shard_map/all_gather | solution.py:259
  186.6 81.2 %copy-start.20 = (f32[2048]{0:T(1024)}, f32[2048]{0:T(1024)S(1)}, u32[]{:S(2)}) copy-start(f32[2048]{0:T(1024)S(1)} %convert_element_type.280) | copy-start | bytes 24580
  186.6 81.2 %copy-start.5 = (bf16[1,128,2048]{2,1,0:T(8,128)(2,1)S(1)}, bf16[1,128,2048]{2,1,0:T(8,128)(2,1)}, u32[]{:S(2)}) copy-start(bf16[1,128,2048]{2,1,0:T(8,128)(2,1)} %param.15) | copy-start | bytes 1572868
  262.8 3.0 copy-start.2
  264.3 4.4 copy-start.26
  265.9 99.0 %copy-start.29 = (f32[128]{0:T(128)}, f32[128]{0:T(128)S(1)}, u32[]{:S(2)}) copy-start(f32[128]{0:T(128)S(1)} %add_rsqrt_fusion) | copy-start | bytes 1540
  267.0 133.8 %all-gather.18.cloned.1.call-start = ((), (), s32[]{:S(2)}) async-start(), calls=%async_computation.14 | async-start | bytes 6488064 | tf_op jit(solution)/shard_map/all_gather | solution.py:202
  267.7 181.2 %all-gather.24.cloned.1.call-start = ((), (), s32[]{:S(2)}) async-start(), calls=%async_computation.18 | async-start | bytes 2621440 | tf_op jit(solution)/shard_map/all_gather | solution.py:260
  267.8 97.1 %copy-start.30 = (f32[128]{0:T(128)}, f32[128]{0:T(128)S(1)}, u32[]{:S(2)}) copy-start(f32[128]{0:T(128)S(1)} %compare_convert_fusion) | copy-start | bytes 1540
  268.8 224.2 %all-gather.22.cloned.1.call-start = ((), (), s32[]{:S(2)}) async-start(), calls=%async_computation.16 | async-start | bytes 6488064 | tf_op jit(solution)/shard_map/all_gather | solution.py:204
  269.5 322.0 %reduce-scatter.14.cloned.1.call-start = ((), (), s32[]{:S(2)}) async-start(), calls=%async_computation.19 | async-start | bytes 5242880 | tf_op jit(solution)/shard_map/reduce_scatter | solution.py:273
  493.0 10.4 copy-start.31
  503.5 3.5 copy-start.35
  503.5 3.5 copy-start.32
  514.7 156.5 %reduce-scatter.12.cloned.1.call-start = ((), (), s32[]{:S(2)}) async-start(), calls=%async_computation.17 | async-start | bytes 5242880 | tf_op jit(solution)/shard_map/reduce_scatter | solution.py:270
  523.5 198.3 %all-gather.26.cloned.1.call-start = ((), (), s32[]{:S(2)}) async-start(), calls=%async_computation.20 | async-start | bytes 2621440 | tf_op jit(solution)/shard_map/all_gather | solution.py:290
  591.6 79.6 %copy-start.3 = (f32[1,128,2048]{2,1,0:T(8,128)S(1)}, f32[1,128,2048]{2,1,0:T(8,128)}, u32[]{:S(2)}) copy-start(f32[1,128,2048]{2,1,0:T(8,128)} %reduce-scatter.14.cloned.1.call-done) | copy-start | bytes 3145732
  675.2 108.2 %reduce-scatter.22.cloned.1.call-start = ((), (), s32[]{:S(2)}) async-start(), calls=%async_computation.24 | async-start | bytes 6488064 | tf_op jit(solution)/shard_map/reduce_scatter | solution.py:359
  683.2 1.4 copy-start.33
  683.2 162.6 %reduce-scatter.24.cloned.1.call-start = ((), (), s32[]{:S(2)}) async-start(), calls=%async_computation.25 | async-start | bytes 6488064 | tf_op jit(solution)/shard_map/reduce_scatter | solution.py:362
  692.1 1.4 copy-start.34
  692.1 216.4 %reduce-scatter.26.cloned.1.call-start = ((), (), s32[]{:S(2)}) async-start(), calls=%async_computation.26 | async-start | bytes 6488064 | tf_op jit(solution)/shard_map/reduce_scatter | solution.py:365
  701.0 20.8 %copy-start.11 = (bf16[8,64,512]{2,1,0:T(8,128)(2,1)S(1)}, bf16[8,64,512]{2,1,0:T(8,128)(2,1)}, u32[]{:S(2)}) copy-start(bf16[8,64,512]{2,1,0:T(8,128)(2,1)} %copy-done.10) | copy-start | bytes 1572868
  701.0 251.9 %reduce-scatter.20.cloned.1.call-start = ((), (), s32[]{:S(2)}) async-start(), calls=%async_computation.23 | async-start | bytes 2359296 | tf_op jit(solution)/shard_map/reduce_scatter | solution.py:356
  726.0 3.5 copy-start.17
  737.4 261.6 %reduce-scatter.16.cloned.1.call-start = ((), (), s32[]{:S(2)}) async-start(), calls=%async_computation.21 | async-start | bytes 2621440 | tf_op jit(solution)/shard_map/reduce_scatter | solution.py:337
  737.7 7.3 copy-start.9
  737.7 7.3 copy-start.13
  737.7 7.3 copy-start.15
  745.0 1.0 copy-start.7
  745.0 2.6 slice-start
  746.0 1.4 copy-start.21
  746.0 3.7 slice-start.1
  747.6 4.8 slice-start.2
  749.7 2.8 slice-start.3
  757.3 306.8 %reduce-scatter.18.cloned.1.call-start = ((), (), s32[]{:S(2)}) async-start(), calls=%async_computation.22 | async-start | bytes 7077888 | tf_op jit(solution)/shard_map/reduce_scatter | solution.py:353
  764.4 234.7 %copy-start.19 = (f32[2048]{0:T(1024)S(1)}, f32[2048]{0:T(1024)}, u32[]{:S(2)}) copy-start(f32[2048]{0:T(1024)} %copy-done.18) | copy-start | bytes 24580
  764.4 234.7 %copy-start.25 = (f32[128]{0:T(128)S(1)}, f32[128]{0:T(128)}, u32[]{:S(2)}) copy-start(f32[128]{0:T(128)} %copy-done.24) | copy-start | bytes 1540
  764.4 234.7 %copy-start.28 = (f32[128]{0:T(128)S(1)}, f32[128]{0:T(128)}, u32[]{:S(2)}) copy-start(f32[128]{0:T(128)} %copy-done.27) | copy-start | bytes 1540
  785.7 214.9 %copy-start.4 = (f32[1,128,2048]{2,1,0:T(8,128)S(1)}, f32[1,128,2048]{2,1,0:T(8,128)}, u32[]{:S(2)}) copy-start(f32[1,128,2048]{2,1,0:T(8,128)} %get-tuple-element.150) | copy-start | bytes 3145732
  848.1 155.1 %copy-start.22 = (f32[2048]{0:T(1024)S(1)}, f32[2048]{0:T(1024)}, u32[]{:S(2)}) copy-start(f32[2048]{0:T(1024)} %get-tuple-element.121) | copy-start | bytes 24580
  848.1 155.1 %copy-start.23 = (f32[2048]{0:T(1024)S(1)}, f32[2048]{0:T(1024)}, u32[]{:S(2)}) copy-start(f32[2048]{0:T(1024)} %get-tuple-element.165) | copy-start | bytes 24580
Sparse Core Ops, SparseCore 0:
  58.9 45.7 all-gather.9
  106.5 44.2 all-gather.11
  152.7 28.1 all-gather.13
  186.0 76.7 reduce-scatter.9
  264.7 43.8 all-gather.19
  310.6 45.9 all-gather.15
  358.7 42.0 all-gather.17
  403.0 45.9 all-gather.23
  451.0 42.0 all-gather.21
  514.8 76.7 reduce-scatter.13
  593.9 77.2 reduce-scatter.11
  675.3 46.4 all-gather.25
  725.6 57.7 reduce-scatter.21
  786.7 59.0 reduce-scatter.23
  849.5 59.0 reduce-scatter.25
  911.7 41.2 reduce-scatter.19
  955.2 43.8 reduce-scatter.15
  1002.3 61.7 reduce-scatter.17
where the time goes:
time: 1080 us; the launch traced here: 1070 us
  waiting for transfers between devices  790 us (73%)
  matrix products  120 us (11%)
  blocking collectives  83 us (8%)
  other arithmetic  42.9 us (4%)
  local copies, waits for them, and re-layouts  19.6 us (2%)
  between operations  15.8 us (1%)
    unnamed x2, blocking collectives  83 us
    reduce_scatter x1, waiting for transfers between devices, per_device(): lax.psum_scatter(mixed_part.reshape(row_count, seq_len, width), 'sp', sca...  76.3 us
    reduce_scatter x1, waiting for transfers between devices, per_device(): lax.psum_scatter(branch_part, 'sp', scatter_dimension=1, tiled=True)  76.2 us
    reduce_scatter x1, waiting for transfers between devices, per_device(): lax.psum_scatter(token_grad_part.reshape(row_count, seq_len, width), 'sp'...  68 us
    reduce_scatter x1, waiting for transfers between devices, per_device(): lax.psum_scatter(mlp_grads[2].astype(jnp.bfloat16), 'dp', scatter_dimensi...  60.4 us
    reduce_scatter x1, waiting for transfers between devices, per_device(): lax.psum_scatter(mlp_grads[1].astype(jnp.bfloat16), 'dp', scatter_dimensi...  60.1 us
    all_gather x1, waiting for transfers between devices, per_device(): lax.all_gather(normed_two.reshape(row_count, slot_count, width), 'sp', ax...  48.1 us
    all_gather x1, waiting for transfers between devices, per_device(): lax.all_gather(qkv_weight, 'dp', axis=0, tiled=True)  46.2 us
  transfers between devices with their start and end apart: 18, of which 18 were waited for; matrix products, arithmetic and copies ran while one was open for 13% of the time, Pallas kernels for 0%

commit v1 on v0

--- a/solution.py
+++ b/solution.py
@@ -1,10 +1,18 @@
+import functools
+
 import jax
 import jax.numpy as jnp
+import numpy as np
 from jax import lax
+from jax.experimental import pallas as pl
+from jax.experimental.pallas import tpu as pltpu
 from jax.sharding import PartitionSpec as P
 
 HEAD_DIM = 64
 ROT = 16
+F32 = jnp.float32
+BF16 = jnp.bfloat16
+MESH = pl.DeviceIdType.MESH
 
 
 eps_norm = 1e-05
@@ -382,6 +390,961 @@
     )
 
 
+def dot_nn(left, right):
+    return lax.dot_general(left, right, (((1,), (0,)), ((), ())), preferred_element_type=F32)
+
+
+def dot_nt(left, right):
+    return lax.dot_general(left, right, (((1,), (1,)), ((), ())), preferred_element_type=F32)
+
+
+def dot_tn(left, right):
+    return lax.dot_general(left, right, (((0,), (0,)), ((), ())), preferred_element_type=F32)
+
+
+def iota(shape, dim):
+    return lax.broadcasted_iota(jnp.int32, shape, dim)
+
+
+def tile(index, size):
+    return pl.ds(pl.multiple_of(index * size, size), size)
+
+
+def normalize(hidden):
+    centre = hidden - jnp.mean(hidden, axis=-1, keepdims=True)
+    rstd = lax.rsqrt(jnp.mean(centre * centre, axis=-1, keepdims=True) + eps_norm)
+    return centre * rstd, rstd
+
+
+class Plan:
+    def __init__(self, dp, sp, slots, width, ff_cols):
+        self.dp, self.sp, self.slots, self.width = dp, sp, slots, width
+        self.chips = dp // 2
+        self.chunk = 2 * slots
+        self.tokens = sp * self.chunk
+        self.seq = sp * slots
+        self.shard = width // dp
+        self.head_cols = width // sp // 2
+        self.pairs = self.head_cols // 128
+        self.qkv_cols = 3 * self.head_cols
+        self.ff_cols = ff_cols
+        lanes = ff_cols // 128
+        self.ff_wide = -(-lanes // 2) * 128
+        self.ff_slim = ff_cols - self.ff_wide
+        self.count_send = 0
+        self.count_recv = 0
+
+    def sems(self, send, recv):
+        at = (self.count_send, self.count_recv)
+        self.count_send += send
+        self.count_recv += recv
+        return at
+
+
+def layer_kernel(plan, sem_at, *refs):
+    (
+        x_in, cot_in, small_in, cos_in, sin_in, wqkv_in, wout_in, wg_in, wu_in, wd_in,
+        out_ref, grad_ref, sums_ref, rg_qkv, rg_out, rg_gate, rg_up, rg_down, n1_hbm,
+        ssem, rsem, lsem,
+        w_qkv, w_out, w_gate, w_up, w_down,
+        buf_a, buf_b, buf_c,
+        part, part_x, part_r, mix, mix_x, mix_r,
+        q_ref, k_ref, v_ref, att, datt, dqkv, raw,
+        act, dgate, dup, kacc, vacc,
+        resid, acc, dres,
+        small, vecs, qbias, lens, colsum, biassum, send_sum, recv_sum, z_sum,
+    ) = refs
+    sp, dp, slots, width, chunk = plan.sp, plan.dp, plan.slots, plan.width, plan.chunk
+    d = lax.axis_index("dp")
+    z = lax.axis_index("sp")
+    c = d % 2
+    oc = 1 - c
+    chip = d // 2
+    sib = (d + 1 - 2 * c, z)
+    first_row = c * slots
+    last = sp - 1
+
+    def remote(src, dst, si, ri, dev):
+        return pltpu.make_async_remote_copy(
+            src_ref=src, dst_ref=dst, send_sem=ssem.at[si], recv_sem=rsem.at[ri],
+            device_id=dev, device_id_type=MESH,
+        )
+
+    def wait_send(src, si):
+        remote(src, src, si, 0, sib).wait_send()
+
+    def wait_recv(dst, ri):
+        remote(dst, dst, 0, ri, sib).wait_recv()
+
+    def block(buf, t, core):
+        return buf.at[pl.ds(pl.multiple_of(t * chunk + core * slots, slots), slots)]
+
+    def rows_of(buf, t):
+        return buf.at[tile(t, chunk)]
+
+    def slot_block(buf, t):
+        return buf.at[tile(t, slots)]
+
+    barrier = pltpu.get_barrier_semaphore()
+    for i in range(1, dp):
+        pl.semaphore_signal(barrier, inc=1, device_id=((d + i) % dp, z), device_id_type=MESH)
+    for i in range(1, sp):
+        pl.semaphore_signal(barrier, inc=1, device_id=(d, (z + i) % sp), device_id_type=MESH)
+    pl.semaphore_wait(barrier, dp + sp - 2)
+
+    class Gather:
+        def __init__(self, name, buf):
+            self.s, self.r = sem_at[name]
+            self.buf = buf
+
+        def start(self, own):
+            s, r = self.s, self.r
+            dst = block(self.buf, z, c)
+
+            @pl.when(z < last)
+            def _():
+                remote(own, dst, s, r + z, (d, z + 1)).start()
+
+            @pl.when(z > 0)
+            def _():
+                remote(own, dst, s + 1, r + z, (d, z - 1)).start()
+
+            remote(own, dst, s + 2 + sp + z, r + sp + z, sib).start()
+
+        def hop(self, k):
+            s, r = self.s, self.r
+            for sign in (-1, 1):
+                t = z + sign * k
+                nxt = z - sign
+                blk = block(self.buf, t, c)
+
+                @pl.when((t >= 0) & (t <= last))
+                def _():
+                    wait_recv(blk, r + t)
+
+                    @pl.when((nxt >= 0) & (nxt <= last))
+                    def _():
+                        remote(blk, blk, s + 2 + t, r + t, (d, nxt)).start()
+
+                    remote(blk, blk, s + 2 + sp + t, r + sp + t, sib).start()
+
+        def need(self, t):
+            wait_recv(block(self.buf, t, oc), self.r + sp + t)
+
+        def drain(self, own):
+            s = self.s
+
+            @pl.when(z < last)
+            def _():
+                wait_send(own, s)
+
+            @pl.when(z > 0)
+            def _():
+                wait_send(own, s + 1)
+
+            for t in range(sp):
+                wait_send(own, s + 2 + sp + t)
+
+                @pl.when(((t < z) & (z < last)) | ((t > z) & (z > 0)))
+                def _():
+                    wait_send(own, s + 2 + t)
+
+    def order(i):
+        low = jnp.minimum(z, last - z)
+        k = jnp.where(i <= 2 * low, (i + 1) // 2, i - low)
+        paired = jnp.where(i % 2 == 1, z - k, z + k)
+        single = jnp.where(z < last - z, z + k, z - k)
+        return jnp.where(i <= 2 * low, paired, single)
+
+    def add_into(dst, terms):
+        @pl.loop(0, slots // 32)
+        def _(i):
+            sl = tile(i, 32)
+            total = dst[sl, :].astype(F32)
+            for term in terms:
+                total = total + term[sl, :].astype(F32)
+            dst[sl, :] = total.astype(dst.dtype)
+
+    class Scatter:
+        def __init__(self, name, parts, from_core, from_line):
+            self.s, self.r = sem_at[name]
+            self.p, self.x, self.l = parts, from_core, from_line
+
+        def core(self, t):
+            remote(
+                block(self.p, t, oc), slot_block(self.x, t), self.s + t, self.r + t, sib
+            ).start()
+
+        def send(self, t, from_end, nbr, slot):
+            mine = block(self.p, t, c)
+            xs = slot_block(self.x, t)
+            wait_recv(xs, self.r + t)
+
+            @pl.when(from_end)
+            def _():
+                add_into(mine, [xs])
+
+            @pl.when(jnp.logical_not(from_end))
+            def _():
+                ls = slot_block(self.l, t)
+                wait_recv(ls, self.r + sp + t)
+                add_into(mine, [xs, ls])
+
+            remote(
+                mine, slot_block(self.l, slot), self.s + sp + t, self.r + sp + slot, (d, nbr)
+            ).start()
+
+        def step(self, n):
+            left = n - (last - z)
+
+            @pl.when((left >= 0) & (left < z))
+            def _():
+                self.send(left, z == last, z - 1, left)
+
+            right = n - z
+
+            @pl.when((right >= 0) & (right < last - z))
+            def _():
+                t = last - right
+                self.send(t, z == 0, z + 1, jnp.where(t == z + 1, sp, t))
+
+        def final(self, total):
+            mine = block(self.p, z, c)
+            xs = slot_block(self.x, z)
+            wait_recv(xs, self.r + z)
+
+            @pl.loop(0, slots // 32)
+            def _(i):
+                sl = tile(i, 32)
+                total[sl, :] = mine[sl, :].astype(F32) + xs[sl, :].astype(F32)
+
+            @pl.when(z < last)
+            def _():
+                ls = slot_block(self.l, z)
+                wait_recv(ls, self.r + sp + z)
+                add_into(total, [ls])
+
+            @pl.when(z > 0)
+            def _():
+                ls = slot_block(self.l, sp)
+                wait_recv(ls, self.r + sp + sp)
+                add_into(total, [ls])
+
+        def drain(self):
+            for t in range(sp):
+                wait_send(slot_block(self.x, t), self.s + t)
+
+                @pl.when(t != z)
+                def _():
+                    wait_send(slot_block(self.x, t), self.s + sp + t)
+
+    def chip_target(q):
+        cx, cy = chip % 2, chip // 2
+        if q % 2:
+            cx = 1 - cx
+        if q // 2:
+            cy = 1 - cy
+        return 2 * cx + 4 * cy
+
+    def weight_window(name, src, core):
+        if name == "out":
+            half = plan.head_cols
+            return src.at[pl.ds(core * half, half), :]
+        if name == "qkv":
+            return src.at[:, pl.ds(core * plan.qkv_cols, plan.qkv_cols)]
+        return src.at[:, pl.ds(core * plan.ff_wide, plan.ff_slim if core else plan.ff_wide)]
+
+    def weight_place(name, dst, owner, core):
+        if name == "out":
+            return dst.at[:, tile(owner, plan.shard)]
+        if name == "qkv":
+            return dst.at[tile(owner, plan.shard), :]
+        return dst.at[tile(owner, plan.shard), pl.ds(0, plan.ff_slim if core else plan.ff_wide)]
+
+    def weight_send(name, src, dst):
+        s, r = sem_at["w_" + name]
+        for q in (1, 2, 3, 0):
+            for core in (0, 1):
+                target = chip_target(q) + core
+                here = weight_window(name, src, core)
+                there = weight_place(name, dst, d, core)
+                if q:
+                    remote(here, there, s + 2 * q + core, r + d, (target, z)).start()
+                else:
+
+                    @pl.when(c != core)
+                    def _():
+                        remote(here, there, s + 2 * q + core, r + d, (target, z)).start()
+
+                    @pl.when(c == core)
+                    def _():
+                        pltpu.make_async_copy(here, there, lsem.at[WEIGHTS.index(name)]).start()
+
+    def weight_wait(name, src, dst):
+        _, r = sem_at["w_" + name]
+        for core in (0, 1):
+
+            @pl.when(c == core)
+            def _():
+                for i in range(1, dp):
+                    other = (d + i) % dp
+                    wait_recv(weight_place(name, dst, other, core), r + other)
+                pltpu.make_async_copy(
+                    weight_window(name, src, core), weight_place(name, dst, d, core),
+                    lsem.at[WEIGHTS.index(name)],
+                ).wait()
+
+    def weight_drain(name, src):
+        s, _ = sem_at["w_" + name]
+        for q in range(4):
+            for core in (0, 1):
+                here = weight_window(name, src, core)
+                if q:
+                    wait_send(here, s + 2 * q + core)
+                else:
+
+                    @pl.when(c != core)
+                    def _():
+                        wait_send(here, s + 2 * q + core)
+
+    def wgrad_piece(name, src, owner, core):
+        if name == "out":
+            return src.at[:, tile(owner, plan.shard)]
+        if name == "qkv":
+            return src.at[tile(owner, plan.shard), :]
+        return src.at[tile(owner, plan.shard), pl.ds(0, plan.ff_slim if core else plan.ff_wide)]
+
+    def wgrad_place(name, dst, from_chip, core):
+        if name == "out":
+            return dst.at[from_chip, pl.ds(core * plan.head_cols, plan.head_cols), :]
+        if name == "qkv":
+            return dst.at[from_chip, :, pl.ds(core * plan.qkv_cols, plan.qkv_cols)]
+        return dst.at[
+            from_chip, :, pl.ds(core * plan.ff_wide, plan.ff_slim if core else plan.ff_wide)
+        ]
+
+    def wgrad_send(name, src, dst):
+        s, r = sem_at["g_" + name]
+        for core in (0, 1):
+
+            @pl.when(c == core)
+            def _():
+                there = wgrad_place(name, dst, chip, core)
+                for q in (1, 2, 3, 0):
+                    for other_core in (0, 1):
+                        target = chip_target(q) + other_core
+                        here = wgrad_piece(name, src, target, core)
+                        if q or other_core != core:
+                            remote(
+                                here, there, s + 2 * q + other_core, r + d, (target, z)
+                            ).start()
+                        else:
+                            pltpu.make_async_copy(
+                                here, there, lsem.at[len(WEIGHTS) + WEIGHTS.index(name)]
+                            ).start()
+
+    def wgrad_finish(name, src, dst):
+        s, r = sem_at["g_" + name]
+        for core in (0, 1):
+
+            @pl.when(c == core)
+            def _():
+                for q in range(4):
+                    for other_core in (0, 1):
+                        target = chip_target(q) + other_core
+                        here = wgrad_piece(name, src, target, core)
+                        if q or other_core != core:
+                            wait_send(here, s + 2 * q + other_core)
+                            wait_recv(
+                                wgrad_place(name, dst, target // 2, other_core), r + target
+                            )
+                        else:
+                            pltpu.make_async_copy(
+                                here, wgrad_place(name, dst, chip, core),
+                                lsem.at[len(WEIGHTS) + WEIGHTS.index(name)],
+                            ).wait()
+
+    gather_x = Gather("ag_x", buf_a)
+    gather_d = Gather("ag_d", buf_c)
+    gather_n = Gather("ag_n", buf_a)
+    gather_b = Gather("ag_b", buf_b)
+    scatter_o = Scatter("rs_o", part, part_x, part_r)
+    scatter_n = Scatter("rs_n", part, part_x, part_r)
+    scatter_i = Scatter("rs_i", part, part_x, part_r)
+    scatter_m = Scatter("rs_m", mix, mix_x, mix_r)
+
+    gather_x.start(x_in)
+    sz, rz = sem_at["sm_z"]
+    sd, rd = sem_at["sm_d"]
+    small[d, z] = small_in[...]
+    for i in range(1, sp):
+        peer = (z + i) % sp
+        remote(small_in, small.at[d, z], sz + i, rz + z, (d, peer)).start()
+    weight_send("qkv", wqkv_in, w_qkv)
+    weight_send("out", wout_in, w_out)
+
+    block(buf_a, z, c)[...] = x_in[...]
+    own_len = small_in[7:8, 0:1]
+
+    @pl.loop(0, slots // 32)
+    def _(i):
+        sl = tile(i, 32)
+        pos = (iota((32, 1), 0) + (z * slots + i * 32)).astype(F32)
+        keep = jnp.where(pos < own_len, 1.0, 0.0)
+        block(buf_c, z, c)[sl, :] = (cot_in[sl, :].astype(F32) * keep).astype(BF16)
+
+    @pl.when(c == 1)
+    def _():
+        pad = plan.ff_wide - plan.ff_slim
+        for ref in (w_gate, w_up, w_down):
+            ref[:, plan.ff_slim :] = jnp.zeros((width, pad), BF16)
+
+    for i in range(1, sp):
+        peer = (z + i) % sp
+        wait_recv(small.at[d, peer], rz + peer)
+    for i in range(1, dp):
+        peer = (d + i) % dp
+        remote(small.at[d], small.at[d], sd + i, rd + d, (peer, z)).start()
+    for i in range(1, dp):
+        peer = (d + i) % dp
+        wait_recv(small.at[peer], rd + peer)
+    per_dp = width // dp // 128
+    for i in range(dp):
+        for h in range(per_dp):
+            at = (i * per_dp + h) * 128
+            vecs[:, at : at + 128] = small[i, 2 * h] + small[i, 2 * h + 1]
+    bias_at = 2 * z + c
+    for h in range(sp // 2):
+        for k in range(3):
+            at = h * 384 + k * 128
+            qbias[0:1, at : at + 128] = (
+                small[bias_at, 2 * h, 4 + k : 5 + k, :] + small[bias_at, 2 * h + 1, 4 + k : 5 + k, :]
+            )
+    for r in range(2):
+        lens[r : r + 1, :] = small[2 * chip + r, 0, 7:8, :]
+
+    n1 = buf_b
+    gain_one, bias_one = vecs[0:1, :], vecs[1:2, :]
+
+    @pl.loop(0, sp)
+    def _(i):
+        @pl.when(i > 0)
+        def _():
+            gather_x.hop(i)
+
+        t = order(i)
+        gather_x.need(t)
+        src, dst = rows_of(buf_a, t), rows_of(n1, t)
+
+        @pl.loop(0, chunk // 32)
+        def _(j):
+            sl = tile(j, 32)
+            unit, _ = normalize(src[sl, :].astype(F32))
+            dst[sl, :] = (unit * vecs[0:1, :] + vecs[1:2, :]).astype(BF16)
+
+    gather_d.start(block(buf_c, z, c))
+    n1_copy = pltpu.make_async_copy(n1, n1_hbm, lsem.at[2 * len(WEIGHTS)])
+    n1_copy.start()
+
+    weight_wait("qkv", wqkv_in, w_qkv)
+    weight_send("gate", wg_in, w_gate)
+    low = iota((1, 128), 1) < 64
+    first_half = iota((1, 128), 1) % 64 < ROT // 2
+
+    def rotated(v, cosine, sine):
+        swapped = jnp.where(
+            first_half, pltpu.roll(v, 128 - ROT // 2, 1), pltpu.roll(v, ROT // 2, 1)
+        )
+        return v * cosine + swapped * sine
+
+    @pl.loop(0, sp)
+    def _(t):
+        src = rows_of(n1, t)
+
+        @pl.loop(0, plan.qkv_cols // 256)
+        def _(n):
+            sl = tile(n, 256)
+            raw[:, sl] = dot_nn(src[...], w_qkv[:, sl]) + qbias[0:1, sl]
+
+        here = tile(t, slots)
+        cosine, sine = cos_in[here, :], sin_in[here, :]
+        for r in range(2):
+            rs = slice(r * slots, (r + 1) * slots)
+            for p in range(plan.pairs):
+                v0 = raw[rs, p * 384 : p * 384 + 128]
+                v1 = raw[rs, p * 384 + 128 : p * 384 + 256]
+                v2 = raw[rs, p * 384 + 256 : p * 384 + 384]
+                r0 = rotated(v0, cosine, sine)
+                r1 = rotated(v1, cosine, sine)
+                r2 = rotated(v2, cosine, sine)
+                q_ref[r, p, here, :] = jnp.where(low, r0, r1).astype(BF16)
+                k_ref[r, p, here, :] = pltpu.roll(jnp.where(low, r2, r0), 64, 1).astype(BF16)
+                v_ref[r, p, here, :] = jnp.where(low, v1, v2).astype(BF16)
+
+    q_rows = min(256, plan.seq)
+    q_blocks = plan.seq // q_rows
+    per_q = q_rows // slots
+    scale = HEAD_DIM ** (-0.5)
+
+    def weights_of(r, p, h, qb):
+        keys_to = (qb + 1) * q_rows
+        mask = low if h == 0 else jnp.logical_not(low)
+        qh = jnp.where(mask, q_ref[r, p, qb * q_rows : keys_to, :], 0).astype(BF16)
+        scores = dot_nt(k_ref[r, p, 0:keys_to, :], qh) * scale
+        key_pos = iota((keys_to, q_rows), 0)
+        query_pos = iota((keys_to, q_rows), 1) + qb * q_rows
+        length = lens[pl.ds(r, 1), 0:1]
+        allowed = (key_pos <= query_pos) & (key_pos.astype(F32) < length)
+        scores = jnp.where(allowed, scores, neg_large)
+        expo = jnp.exp(scores - jnp.max(scores, axis=0, keepdims=True))
+        return expo * (1.0 / jnp.sum(expo, axis=0, keepdims=True))
+
+    def att_rows(r, t):
+        return pl.ds(pl.multiple_of(t * chunk + r * slots, slots), slots)
+
+    def attention(r, p):
+        for qb in range(q_blocks):
+            outs = []
+            for h in range(2):
+                probs = weights_of(r, p, h, qb).astype(BF16)
+                outs.append(dot_tn(probs, v_ref[r, p, 0 : (qb + 1) * q_rows, :]))
+            both = jnp.where(low, outs[0], outs[1]).astype(BF16)
+            for i in range(per_q):
+                att[att_rows(r, qb * per_q + i), p * 128 : (p + 1) * 128] = both[
+                    i * slots : (i + 1) * slots
+                ]
+
+    @pl.loop(0, 2)
+    def _(r):
+        for p in range(plan.pairs):
+            attention(r, p)
+
+    gather_d.hop(1)
+    gather_x.drain(x_in)
+
+    weight_wait("out", wout_in, w_out)
+    weight_send("up", wu_in, w_up)
+    weight_send("down", wd_in, w_down)
+
+    def far_first(i):
+        return jnp.where(z < last - z, last - i, i)
+
+    @pl.loop(0, sp)
+    def _(i):
+        t = far_first(i)
+        src, dst = rows_of(att, t), rows_of(part, t)
+
+        @pl.loop(0, width // 256)
+        def _(n):
+            sl = tile(n, 256)
+            dst[:, sl] = dot_nn(src[...], w_out[:, sl]).astype(BF16)
+
+        scatter_o.core(t)
+
+    scatter_o.step(0)
+    for k in range(1, sp - 1):
+        scatter_o.step(k)
+        gather_d.hop(k + 1)
+    scatter_o.final(acc)
+
+    own_n = block(buf_a, z, c)
+
+    @pl.loop(0, slots // 32)
+    def _(i):
+        sl = tile(i, 32)
+        hidden = x_in[sl, :].astype(F32) + acc[sl, :]
+        resid[sl, :] = hidden
+        unit, _ = normalize(hidden)
+        own_n[sl, :] = (unit * vecs[2:3, :] + vecs[3:4, :]).astype(BF16)
+
+    gather_n.start(own_n)
+    for i in range(sp):
+        gather_d.need(i)
+    scatter_o.drain()
+    n1_copy.wait()
+
+    weight_wait("gate", wg_in, w_gate)
+    weight_wait("up", wu_in, w_up)
+    weight_wait("down", wd_in, w_down)
+
+    @pl.loop(0, sp)
+    def _(i):
+        @pl.when(i > 0)
+        def _():
+            gather_n.hop(i)
+
+        t = order(i)
+        gather_n.need(t)
+        tok, gout = rows_of(buf_a, t), rows_of(buf_c, t)
+        act_t, dg_t, du_t = rows_of(act, t), rows_of(dgate, t), rows_of(dup, t)
+        part_t, mix_t = rows_of(part, t), rows_of(mix, t)
+
+        @pl.loop(0, plan.ff_wide // 256)
+        def _(n):
+            sl = tile(n, 256)
+            gate = dot_nn(tok[...], w_gate[:, sl])
+            up = dot_nn(tok[...], w_up[:, sl])
+            d_act = dot_nn(gout[...], w_down[:, sl])
+            sig = jax.nn.sigmoid(gate)
+            silu = gate * sig
+            act_t[:, sl] = (silu * up).astype(BF16)
+            du_t[:, sl] = (d_act * silu).astype(BF16)
+            dg_t[:, sl] = (d_act * up * sig * (1.0 + gate * (1.0 - sig))).astype(BF16)
+
+        @pl.loop(0, width // 256)
+        def _(n):
+            sl = tile(n, 256)
+            part_t[:, sl] = (
+                dot_nt(dg_t[...], w_gate[sl, :]) + dot_nt(du_t[...], w_up[sl, :])
+            ).astype(BF16)
+            mix_t[:, sl] = dot_nt(act_t[...], w_down[sl, :]).astype(BF16)
+
+        scatter_n.core(t)
+        scatter_m.core(t)
+
+    def wgrad(tokens, cols, dst):
+        @pl.loop(0, width // 256)
+        def _(n):
+            sl = tile(n, 256)
+            dst[sl, :] = dot_tn(tokens[:, sl], cols[...]).astype(BF16)
+
+    scatter_n.step(0)
+    weight_drain("down", wd_in)
+    wgrad(buf_c, act, w_down)
+    wgrad_send("down", w_down, rg_down)
+    scatter_n.step(1)
+    wgrad(buf_a, dgate, w_gate)
+    wgrad_send("gate", w_gate, rg_gate)
+    for k in range(2, sp - 1):
+        scatter_n.step(k)
+    wgrad(buf_a, dup, w_up)
+    wgrad_send("up", w_up, rg_up)
+    scatter_n.final(acc)
+
+    gather_n.drain(own_n)
+    n1_back = pltpu.make_async_copy(n1_hbm, buf_a, lsem.at[2 * len(WEIGHTS) + 1])
+    n1_back.start()
+    colsum[...] = jnp.zeros_like(colsum)
+    own_d, own_b = block(buf_c, z, c), block(buf_b, z, c)
+
+    def norm_back(grad, hidden, gain, row):
+        unit, rstd = normalize(hidden)
+        colsum[row : row + 1, :] += jnp.sum(grad * unit, axis=0, keepdims=True)
+        colsum[row + 1 : row + 2, :] += jnp.sum(grad, axis=0, keepdims=True)
+        scaled = grad * gain
+        return rstd * (
+            scaled
+            - jnp.mean(scaled, axis=-1, keepdims=True)
+            - unit * jnp.mean(scaled * unit, axis=-1, keepdims=True)
+        )
+
+    @pl.loop(0, slots // 32)
+    def _(i):
+        sl = tile(i, 32)
+        back = own_d[sl, :].astype(F32) + norm_back(acc[sl, :], resid[sl, :], vecs[2:3, :], 2)
+        dres[sl, :] = back
+        own_b[sl, :] = back.astype(BF16)
+
+    gather_b.start(own_b)
+    scatter_n.drain()
+    scatter_m.step(0)
+
+    @pl.loop(0, sp)
+    def _(i):
+        @pl.when(i > 0)
+        def _():
+            gather_b.hop(i)
+
+        @pl.when((i > 0) & (i < last))
+        def _():
+            scatter_m.step(i)
+
+        t = order(i)
+        gather_b.need(t)
+        datt[tile(t, chunk), :] = dot_nt(rows_of(buf_b, t)[...], w_out[...]).astype(BF16)
+
+    biassum[...] = jnp.zeros_like(biassum)
+
+    def attention_back(r, p):
+        cols = slice(p * 128, (p + 1) * 128)
+        for qb in range(q_blocks):
+            keys_to = (qb + 1) * q_rows
+            dav = jnp.concatenate(
+                [datt[att_rows(r, qb * per_q + i), cols] for i in range(per_q)], axis=0
+            )
+            qv = q_ref[r, p, qb * q_rows : keys_to, :]
+            dq, dk, dv = [], [], []
+            for h in range(2):
+                mask = low if h == 0 else jnp.logical_not(low)
+                probs = weights_of(r, p, h, qb)
+                dprobs = dot_nt(v_ref[r, p, 0:keys_to, :], jnp.where(mask, dav, 0).astype(BF16))
+                delta = jnp.sum(dprobs * probs, axis=0, keepdims=True)
+                dscores = (probs * (dprobs - delta)).astype(BF16)
+                dv.append(dot_nn(probs.astype(BF16), dav))
+                dk.append(dot_nn(dscores, qv))
+                dq.append(dot_tn(dscores, k_ref[r, p, 0:keys_to, :]))
+            dq_both = (jnp.where(low, dq[0], dq[1]) * scale).astype(BF16)
+            dk_both = jnp.where(low, dk[0], dk[1])
+            dv_both = jnp.where(low, dv[0], dv[1])
+            if qb == 0:
+                kacc[0:keys_to, :] = dk_both
+                vacc[0:keys_to, :] = dv_both
+            else:
+                kept = keys_to - q_rows
+                kacc[0:kept, :] += dk_both[0:kept]
+                vacc[0:kept, :] += dv_both[0:kept]
+                kacc[kept:keys_to, :] = dk_both[kept:keys_to]
+                vacc[kept:keys_to, :] = dv_both[kept:keys_to]
+            q_ref[r, p, qb * q_rows : keys_to, :] = dq_both
+        for t in range(sp):
+            ts = slice(t * slots, (t + 1) * slots)
+            dqv = q_ref[r, p, ts, :].astype(F32)
+            dkv = (kacc[ts, :] * scale).astype(BF16).astype(F32)
+            dvv = vacc[ts, :].astype(BF16).astype(F32)
+            swapped = pltpu.roll(dkv, 64, 1)
+            cosine, sine = cos_in[ts, :], -sin_in[ts, :]
+            g0 = rotated(jnp.where(low, dqv, swapped), cosine, sine)
+            g1 = jnp.where(low, dvv, rotated(dqv, cosine, sine))
+            g2 = jnp.where(low, rotated(swapped, cosine, sine), dvv)
+            for k, g in enumerate((g0, g1, g2)):
+                g = g.astype(BF16)
+                dqkv[att_rows(r, t), p * 384 + k * 128 : p * 384 + (k + 1) * 128] = g
+                row = 3 * p + k
+                biassum[row : row + 1, :] += jnp.sum(g.astype(F32), axis=0, keepdims=True)
+
+    @pl.loop(0, 2)
+    def _(r):
+        for p in range(plan.pairs):
+            attention_back(r, p)
+
+    @pl.loop(0, sp)
+    def _(i):
+        t = far_first(i)
+        dst, src = rows_of(part, t), rows_of(dqkv, t)
+
+        @pl.loop(0, width // 256)
+        def _(n):
+            sl = tile(n, 256)
+            dst[:, sl] = dot_nt(src[...], w_qkv[sl, :]).astype(BF16)
+
+        scatter_i.core(t)
+
+    scatter_i.step(0)
+    n1_back.wait()
+    wgrad(buf_a, dqkv, w_qkv)
+    wgrad_send("qkv", w_qkv, rg_qkv)
+    scatter_i.step(1)
+
+    @pl.loop(0, width // 256)
+    def _(n):
+        sl = tile(n, 256)
+        w_out[:, sl] = dot_tn(att[...], buf_b[:, sl]).astype(BF16)
+
+    wgrad_send("out", w_out, rg_out)
+    for k in range(2, sp - 1):
+        scatter_i.step(k)
+    scatter_m.final(acc)
+
+    @pl.loop(0, slots // 32)
+    def _(i):
+        sl = tile(i, 32)
+        pos = (iota((32, 1), 0) + (z * slots + i * 32)).astype(F32)
+        keep = jnp.where(pos < small_in[7:8, 0:1], 1.0, 0.0)
+        out_ref[sl, :] = (keep * (resid[sl, :] + acc[sl, :])).astype(BF16)
+
+    scatter_i.final(acc)
+
+    @pl.loop(0, slots // 32)
+    def _(i):
+        sl = tile(i, 32)
+        back = norm_back(acc[sl, :], x_in[sl, :].astype(F32), vecs[0:1, :], 0)
+        grad_ref[sl, :] = dres[sl, :] + back
+
+    per = plan.shard
+    for i in range(dp):
+        send_sum[i, :, 0:per] = colsum[:, i * per : (i + 1) * per]
+        send_sum[i, :, per : per + 128] = biassum[...]
+    sa, ra = sem_at["su_d"]
+    sb, rb = sem_at["su_z"]
+    recv_sum[d] = send_sum[d]
+    for i in range(1, dp):
+        peer = (d + i) % dp
+        remote(send_sum.at[peer], recv_sum.at[d], sa + i, ra + d, (peer, z)).start()
+    for i in range(1, dp):
+        peer = (d + i) % dp
+        wait_recv(recv_sum.at[peer], ra + peer)
+    norm_total = recv_sum[0, :, 0:per]
+    for i in range(1, dp):
+        norm_total = norm_total + recv_sum[i, :, 0:per]
+    bias_total = recv_sum[c, :, per : per + 128]
+    for i in range(1, dp // 2):
+        bias_total = bias_total + recv_sum[2 * i + c, :, per : per + 128]
+    z_sum[z, :, 0:per] = norm_total
+    z_sum[z, :, per : per + 128] = bias_total
+    for i in range(1, sp):
+        peer = (z + i) % sp
+        remote(z_sum.at[z], z_sum.at[z], sb + i, rb + z, (d, peer)).start()
+    for i in range(1, sp):
+        peer = (z + i) % sp
+        wait_recv(z_sum.at[peer], rb + peer)
+    norm_total = z_sum[0, :, 0:per]
+    for i in range(1, sp):
+        norm_total = norm_total + z_sum[i, :, 0:per]
+    sums_ref[:, 0:per] = norm_total
+    sums_ref[:, per : per + 128] = z_sum[chip, :, per : per + 128]
+
+    for name, src, dst in (
+        ("down", w_down, rg_down), ("gate", w_gate, rg_gate), ("up", w_up, rg_up),
+        ("qkv", w_qkv, rg_qkv), ("out", w_out, rg_out),
+    ):
+        wgrad_finish(name, src, dst)
+    for name, src in (("qkv", wqkv_in), ("out", wout_in), ("gate", wg_in), ("up", wu_in)):
+        weight_drain(name, src)
+    gather_d.drain(own_d)
+    gather_b.drain(own_b)
+    scatter_m.drain()
+    scatter_i.drain()
+    for i in range(1, sp):
+        wait_send(small_in, sz + i)
+        wait_send(z_sum.at[z], sb + i)
+    for i in range(1, dp):
+        wait_send(small.at[d], sd + i)
+        wait_send(send_sum.at[0], sa + i)
+
+
+WEIGHTS = ("qkv", "out", "gate", "up", "down")
+
+
+def rotary_lanes(seq_len):
+    half = ROT // 2
+    freq = theta ** (-(np.arange(half, dtype=np.float32) * np.float32(2.0)) / np.float32(ROT))
+    angles = np.arange(seq_len, dtype=np.float32)[:, None] * freq.astype(np.float32)[None, :]
+    cosine, sine = np.cos(angles), np.sin(angles)
+    cos_head = np.ones((seq_len, HEAD_DIM), np.float32)
+    sin_head = np.zeros((seq_len, HEAD_DIM), np.float32)
+    cos_head[:, :half], cos_head[:, half:ROT] = cosine, cosine
+    sin_head[:, :half], sin_head[:, half:ROT] = -sine, sine
+    return np.tile(cos_head, (1, 2)), np.tile(sin_head, (1, 2))
+
+
+def per_device_fast(
+    layer_input, lengths, cotangent, ln1_gain, ln1_bias, ln2_gain, ln2_bias,
+    qkv_weight, qkv_bias, out_weight, gate_weight, up_weight, down_weight,
+):
+    dp, sp = lax.axis_size("dp"), lax.axis_size("sp")
+    z = lax.axis_index("sp")
+    _, slots, width = layer_input.shape
+    plan = Plan(dp, sp, slots, width, gate_weight.shape[1])
+    sem_at = {}
+    for name in WEIGHTS:
+        sem_at["w_" + name] = plan.sems(8, dp)
+        sem_at["g_" + name] = plan.sems(8, dp)
+    for name in ("ag_x", "ag_d", "ag_n", "ag_b"):
+        sem_at[name] = plan.sems(2 + 2 * sp, 2 * sp)
+    for name in ("rs_o", "rs_n", "rs_i", "rs_m"):
+        sem_at[name] = plan.sems(2 * sp, 2 * sp + 1)
+    for name in ("sm_z", "su_z"):
+        sem_at[name] = plan.sems(sp, sp)
+    for name in ("sm_d", "su_d"):
+        sem_at[name] = plan.sems(dp, dp)
+
+    even = z % 2 == 0
+    norms = jnp.stack([ln1_gain, ln1_bias, ln2_gain, ln2_bias]).astype(F32)
+    none = jnp.zeros_like(norms)
+    norm_rows = jnp.where(
+        even, jnp.concatenate([norms, none], 1), jnp.concatenate([none, norms], 1)
+    )
+    bias = qkv_bias.astype(F32)
+    none = jnp.zeros_like(bias)
+    bias_rows = jnp.where(
+        even, jnp.concatenate([bias, none]), jnp.concatenate([none, bias])
+    ).reshape(3, 128)
+    len_row = jnp.broadcast_to(lengths.astype(F32)[:, None], (1, 128))
+    small = jnp.concatenate([norm_rows, bias_rows, len_row], axis=0)
+    cosine, sine = rotary_lanes(sp * slots)
+
+    vmem = pl.BlockSpec(memory_space=pltpu.VMEM)
+    hbm = pl.BlockSpec(memory_space=pl.ANY)
+    out_shape = [
+        jax.ShapeDtypeStruct((slots, width), BF16),
+        jax.ShapeDtypeStruct((slots, width), F32),
+        jax.ShapeDtypeStruct((8, plan.shard + 128), F32),
+        jax.ShapeDtypeStruct((plan.chips,) + qkv_weight.shape, BF16),
+        jax.ShapeDtypeStruct((plan.chips,) + out_weight.shape, BF16),
+        jax.ShapeDtypeStruct((plan.chips,) + gate_weight.shape, BF16),
+        jax.ShapeDtypeStruct((plan.chips,) + up_weight.shape, BF16),
+        jax.ShapeDtypeStruct((plan.chips,) + down_weight.shape, BF16),
+        jax.ShapeDtypeStruct((plan.tokens, width), BF16),
+    ]
+    tokens, heads, ff = plan.tokens, plan.head_cols, plan.ff_wide
+    scratch = [
+        pltpu.SemaphoreType.DMA((plan.count_send,)),
+        pltpu.SemaphoreType.DMA((plan.count_recv,)),
+        pltpu.SemaphoreType.DMA((2 * len(WEIGHTS) + 2,)),
+        pltpu.VMEM((width, plan.qkv_cols), BF16),
+        pltpu.VMEM((heads, width), BF16),
+        pltpu.VMEM((width, ff), BF16),
+        pltpu.VMEM((width, ff), BF16),
+        pltpu.VMEM((width, ff), BF16),
+        pltpu.VMEM((tokens, width), BF16),
+        pltpu.VMEM((tokens, width), BF16),
+        pltpu.VMEM((tokens, width), BF16),
+        pltpu.VMEM((tokens, width), BF16),
+        pltpu.VMEM((sp * slots, width), BF16),
+        pltpu.VMEM(((sp + 1) * slots, width), BF16),
+        pltpu.VMEM((tokens, width), BF16),
+        pltpu.VMEM((sp * slots, width), BF16),
+        pltpu.VMEM(((sp + 1) * slots, width), BF16),
+        pltpu.VMEM((2, plan.pairs, plan.seq, 128), BF16),
+        pltpu.VMEM((2, plan.pairs, plan.seq, 128), BF16),
+        pltpu.VMEM((2, plan.pairs, plan.seq, 128), BF16),
+        pltpu.VMEM((tokens, heads), BF16),
+        pltpu.VMEM((tokens, heads), BF16),
+        pltpu.VMEM((tokens, plan.qkv_cols), BF16),
+        pltpu.VMEM((plan.chunk, plan.qkv_cols), F32),
+        pltpu.VMEM((tokens, ff), BF16),
+        pltpu.VMEM((tokens, ff), BF16),
+        pltpu.VMEM((tokens, ff), BF16),
+        pltpu.VMEM((plan.seq, 128), F32),
+        pltpu.VMEM((plan.seq, 128), F32),
+        pltpu.VMEM((slots, width), F32),
+        pltpu.VMEM((slots, width), F32),
+        pltpu.VMEM((slots, width), F32),
+        pltpu.VMEM((dp, sp, 8, 128), F32),
+        pltpu.VMEM((8, width), F32),
+        pltpu.VMEM((8, plan.qkv_cols), F32),
+        pltpu.VMEM((8, 128), F32),
+        pltpu.VMEM((8, width), F32),
+        pltpu.VMEM((8, 128), F32),
+        pltpu.VMEM((dp, 8, plan.shard + 128), F32),
+        pltpu.VMEM((dp, 8, plan.shard + 128), F32),
+        pltpu.VMEM((sp, 8, plan.shard + 128), F32),
+    ]
+    outs = pl.pallas_call(
+        functools.partial(layer_kernel, plan, sem_at),
+        out_shape=out_shape,
+        in_specs=[vmem] * 5 + [hbm] * 5,
+        out_specs=[vmem] * 3 + [hbm] * 6,
+        scratch_shapes=scratch,
+        compiler_params=pltpu.CompilerParams(
+            collective_id=0, has_side_effects=True, vmem_limit_bytes=63 * 1024 * 1024
+        ),
+    )(
+        layer_input[0], cotangent[0], small, jnp.asarray(cosine), jnp.asarray(sine),
+        qkv_weight, out_weight, gate_weight, up_weight, down_weight,
+    )
+    sums = outs[2]
+    own = lax.dynamic_slice_in_dim(sums[:4, : plan.shard], z * (plan.shard // sp), plan.shard // sp, 1)
+    bias_grad = lax.dynamic_slice_in_dim(
+        sums[:, plan.shard :].reshape(-1), z * qkv_bias.shape[0], qkv_bias.shape[0]
+    )
+    grads = [jnp.sum(g.astype(F32), axis=0) for g in outs[3:8]]
+    return (
+        outs[0][None], outs[1][None], own[0], own[1], own[2], own[3],
+        grads[0], bias_grad, grads[1], grads[2], grads[3], grads[4],
+    )
+
+
 def solution(mesh):
     placed = (
         P("dp", "sp", None),
@@ -398,8 +1361,9 @@
         P("dp", "sp"),
         P("dp", "sp"),
     )
+    fast = mesh.shape["dp"] == 8 and mesh.shape["sp"] == 4
     return jax.shard_map(
-        per_device,
+        per_device_fast if fast else per_device,
         mesh=mesh,
         in_specs=placed,
         out_specs=(

time: 1080 us -> 397 us (0.37)
  waiting for transfers between devices: 790 us -> 0 us
  Pallas kernels: 0 us -> 379 us
  matrix products: 120 us -> 0 us
  blocking collectives: 83 us -> 0 us
  other arithmetic: 42.9 us -> 11.9 us
  local copies, waits for them, and re-layouts: 19.6 us -> 3.87 us
  between operations: 15.8 us -> 1.34 us
    reduce_scatter x9 -> x0, waiting for transfers between devices: 464 us -> none  [the longest x1 76.3 us: per_device(): lax.psum_scatter(mixed_part.reshape(row_count, seq_len, width), 'sp', sca...]
    pallas_call x0 -> x1, Pallas kernels: none -> 379 us  [per_device_fast(): pl.pallas_call(functools.partial(layer_kernel, plan, sem_at), out_shape=o...]
    all_gather x9 -> x0, waiting for transfers between devices: 323 us -> none  [the longest x1 48.1 us: per_device(): lax.all_gather(normed_two.reshape(row_count, slot_count, width), 'sp', ax...]
    dot_general x21 -> x0, matrix products: 120 us -> none  [the longest x5 34.2 us: contract_rows(): lax.dot_general(left, right, (((0,), (0,)), ((), ())), preferred_element_...]
    unnamed x2 -> x0, blocking collectives: 83 us -> none
    convert_element_type x17 -> x2, other arithmetic: 26.8 us -> 1.37 us  [the longest x1 0.72 us: per_device_fast(): norms = jnp.stack([ln1_gain, ln1_bias, ln2_gain, ln2_bias]).astype(F32)]
  transfers between devices with their start and end apart: 18 -> 0, of which waited for: 18 -> 0; matrix products, arithmetic and copies ran while one was open for 13% -> 0% of each run, Pallas kernels for 0% -> 0%
where the time goes in v1:
time: 397 us
  Pallas kernels  379 us (95%)
  other arithmetic  11.9 us (3%)
    pallas_call x1, Pallas kernels, per_device_fast(): pl.pallas_call(functools.partial(layer_kernel, plan, sem_at), out_shape=o...  379 us
    reduce_sum x4, other arithmetic, per_device_fast(): grads = [jnp.sum(g.astype(F32), axis=0) for g in outs[3:8]]  9.67 us

profile of v1, /device:TPU:0, one launch (start us, length us, event | category | flops | bytes accessed | tf_op | source)
XLA Modules:
  0.0 396.5 jit_solution(12433555229409088712)
XLA Ops:
  0.7 0.7 maximum_convert_fusion
  1.4 0.1 pad_select_fusion
  1.4 0.7 convert_element_type.25
  2.1 0.1 select_bitcast_fusion
  2.8 0.1 pad.6.clone
  2.9 0.7 maximum_maximum_fusion.refs_2_
  3.6 379.4 %shard_map.238 = (bf16[128,2048]{1,0:T(8,128)(2,1)}, f32[128,2048]{1,0:T(8,128)}, f32[8,384]{1,0:T(8,128)}, bf16[4,256,1536]{2,1,0:T(8,128)(2,1)}, bf16[4,512,25...) custom-call(bf16[128,2048]{1,0:T(8,128)(2,1)} %bitcast.23, ...), custom_call_target="tpu_custom_call" | custom-call | tf_op jit(solution)/shard_map/pallas_call | solution.py:1323
  383.0 0.0 copy-start
  383.0 5.6 %convert_reduce_fusion.1 = (f32[256,1408]{1,0:T(8,128)}, f32[256,1408]{1,0:T(8,128)}) fusion(bf16[4,256,1408]{2,1,0:T(8,128)(2,1)} %get-tuple-element.27, bf16[4,256,1408]{2,1,0:T(8,128)(2,1)} %get-tuple-element.26), kind=kLoop, calls=%fused_computation.1 | loop fusion | flops 5046272 | bytes 8650752 | tf_op jit(solution)/shard_map/reduce_sum | solution.py:1341
  388.6 0.0 copy-start.1
  388.6 0.0 copy-done
  388.6 1.6 convert_reduce_fusion
  390.2 0.0 copy-start.2
  390.2 0.8 copy-done.1
  391.0 0.0 copy-start.5
  391.0 0.0 copy-start.4
  391.0 0.0 copy-start.3
  391.0 1.5 convert_reduce_fusion.3
  392.6 0.0 copy-done.2
  392.6 0.9 convert_reduce_fusion.4
  393.5 0.0 copy-done.5
  393.5 0.1 constant_dynamic-slice_fusion
  393.6 0.5 slice_bitcast_fusion.1
  394.1 0.6 dynamic_slice.7
  394.7 0.0 copy-done.4
  394.7 0.8 copy.30
  395.5 0.0 copy-done.3
  395.5 1.0 copy.31
  (2 shorter events, 0.0 us)
Async XLA Ops:
  383.0 5.6 %copy-start = (bf16[4,256,1536]{2,1,0:T(8,128)(2,1)S(1)}, bf16[4,256,1536]{2,1,0:T(8,128)(2,1)}, u32[]{:S(2)}) copy-start(bf16[4,256,1536]{2,1,0:T(8,128)(2,1)} %get-tuple-element.23) | copy-start | bytes 9437188
  388.6 2.4 copy-start.1
  390.2 2.3 copy-start.2
  391.0 2.5 copy-start.5
  391.0 3.7 copy-start.4
  391.0 4.5 %copy-start.3 = (f32[128,2048]{1,0:T(8,128)S(1)}, f32[128,2048]{1,0:T(8,128)}, u32[]{:S(2)}) copy-start(f32[128,2048]{1,0:T(8,128)} %get-tuple-element.21) | copy-start | bytes 3145732

commit v2 on v1

--- a/solution.py
+++ b/solution.py
@@ -449,10 +449,11 @@
         w_qkv, w_out, w_gate, w_up, w_down,
         buf_a, buf_b, buf_c,
         part, part_x, part_r, mix, mix_x, mix_r,
-        q_ref, k_ref, v_ref, att, datt, dqkv, raw,
+        q_ref, k_ref, v_ref, att, raw,
         act, dgate, dup, kacc, vacc,
         resid, acc, dres,
         small, vecs, qbias, lens, colsum, biassum, send_sum, recv_sum, z_sum,
+        st_qkv, st_out, st_gate, st_up, st_down,
     ) = refs
     sp, dp, slots, width, chunk = plan.sp, plan.dp, plan.slots, plan.width, plan.chunk
     d = lax.axis_index("dp")
@@ -663,7 +664,7 @@
 
     def weight_send(name, src, dst):
         s, r = sem_at["w_" + name]
-        for q in (1, 2, 3, 0):
+        for q in (1, 2, 0):
             for core in (0, 1):
                 target = chip_target(q) + core
                 here = weight_window(name, src, core)
@@ -674,38 +675,57 @@
 
                     @pl.when(c != core)
                     def _():
-                        remote(here, there, s + 2 * q + core, r + d, (target, z)).start()
+                        remote(here, there, s + core, r + d, (target, z)).start()
 
                     @pl.when(c == core)
                     def _():
                         pltpu.make_async_copy(here, there, lsem.at[WEIGHTS.index(name)]).start()
 
+    def weight_forward(name, dst):
+        s, r = sem_at["w_" + name]
+        for core in (0, 1):
+
+            @pl.when(c == core)
+            def _():
+                for k in (0, 1):
+                    owner = chip_target(1 if core else 2) + k
+                    place = weight_place(name, dst, owner, core)
+                    wait_recv(place, r + owner)
+                    target = chip_target(2 if core else 1) + core
+                    remote(place, place, s + 6 + k, r + owner, (target, z)).start()
+
     def weight_wait(name, src, dst):
         _, r = sem_at["w_" + name]
         for core in (0, 1):
 
             @pl.when(c == core)
             def _():
-                for i in range(1, dp):
-                    other = (d + i) % dp
-                    wait_recv(weight_place(name, dst, other, core), r + other)
+                for q in (0, 2 if core else 1, 3):
+                    for k in (0, 1):
+                        if q or k != core:
+                            owner = chip_target(q) + k
+                            wait_recv(weight_place(name, dst, owner, core), r + owner)
                 pltpu.make_async_copy(
                     weight_window(name, src, core), weight_place(name, dst, d, core),
                     lsem.at[WEIGHTS.index(name)],
                 ).wait()
 
-    def weight_drain(name, src):
+    def weight_drain(name, src, dst):
         s, _ = sem_at["w_" + name]
-        for q in range(4):
-            for core in (0, 1):
-                here = weight_window(name, src, core)
-                if q:
-                    wait_send(here, s + 2 * q + core)
-                else:
-
-                    @pl.when(c != core)
-                    def _():
-                        wait_send(here, s + 2 * q + core)
+        for core in (0, 1):
+            here = weight_window(name, src, core)
+            wait_send(here, s + 2 + core)
+            wait_send(here, s + 4 + core)
+
+            @pl.when(c != core)
+            def _():
+                wait_send(here, s + core)
+
+            @pl.when(c == core)
+            def _():
+                place = weight_place(name, dst, d, core)
+                wait_send(place, s + 6)
+                wait_send(place, s + 7)
 
     def wgrad_piece(name, src, owner, core):
         if name == "out":
@@ -714,34 +734,69 @@
             return src.at[tile(owner, plan.shard), :]
         return src.at[tile(owner, plan.shard), pl.ds(0, plan.ff_slim if core else plan.ff_wide)]
 
-    def wgrad_place(name, dst, from_chip, core):
+    def wgrad_place(name, dst, slot, core):
         if name == "out":
-            return dst.at[from_chip, pl.ds(core * plan.head_cols, plan.head_cols), :]
+            return dst.at[slot, pl.ds(core * plan.head_cols, plan.head_cols), :]
         if name == "qkv":
-            return dst.at[from_chip, :, pl.ds(core * plan.qkv_cols, plan.qkv_cols)]
-        return dst.at[
-            from_chip, :, pl.ds(core * plan.ff_wide, plan.ff_slim if core else plan.ff_wide)
-        ]
-
-    def wgrad_send(name, src, dst):
+            return dst.at[slot, :, pl.ds(core * plan.qkv_cols, plan.qkv_cols)]
+        return dst.at[slot, :, pl.ds(core * plan.ff_wide, plan.ff_slim if core else plan.ff_wide)]
+
+    def stage_place(name, stage, k, core):
+        if name in ("out", "qkv"):
+            return stage.at[k]
+        return stage.at[k, :, pl.ds(0, plan.ff_slim if core else plan.ff_wide)]
+
+    def wgrad_send(name, src, dst, stage):
         s, r = sem_at["g_" + name]
         for core in (0, 1):
+            near = 1 if core else 2
 
             @pl.when(c == core)
             def _():
-                there = wgrad_place(name, dst, chip, core)
-                for q in (1, 2, 3, 0):
-                    for other_core in (0, 1):
-                        target = chip_target(q) + other_core
-                        here = wgrad_piece(name, src, target, core)
-                        if q or other_core != core:
-                            remote(
-                                here, there, s + 2 * q + other_core, r + d, (target, z)
-                            ).start()
-                        else:
-                            pltpu.make_async_copy(
-                                here, there, lsem.at[len(WEIGHTS) + WEIGHTS.index(name)]
-                            ).start()
+                for k in (0, 1):
+                    remote(
+                        wgrad_piece(name, src, chip_target(3) + k, core),
+                        stage_place(name, stage, k, core),
+                        s + k, r + 6 + k, (chip_target(near) + core, z),
+                    ).start()
+                for k in (0, 1):
+                    target = chip_target(near) + k
+                    remote(
+                        wgrad_piece(name, src, target, core),
+                        wgrad_place(name, dst, near, core),
+                        s + 2 + k, r + 2 * near + core, (target, z),
+                    ).start()
+                remote(
+                    wgrad_piece(name, src, d + 1 - 2 * core, core),
+                    wgrad_place(name, dst, 0, core), s + 4, r + core, sib,
+                ).start()
+                pltpu.make_async_copy(
+                    wgrad_piece(name, src, d, core), wgrad_place(name, dst, 0, core),
+                    lsem.at[len(WEIGHTS) + WEIGHTS.index(name)],
+                ).start()
+
+    def wgrad_merge(name, src, dst, stage):
+        s, r = sem_at["g_" + name]
+        for core in (0, 1):
+            far = 2 if core else 1
+
+            @pl.when(c == core)
+            def _():
+                for k in (0, 1):
+                    target = chip_target(far) + k
+                    came = stage_place(name, stage, k, core)
+                    mine = wgrad_piece(name, src, target, core)
+                    wait_recv(came, r + 6 + k)
+
+                    @pl.loop(0, came.shape[0] // 32)
+                    def _(i):
+                        sl = tile(i, 32)
+                        mine[sl, :] = (mine[sl, :].astype(F32) + came[sl, :].astype(F32)).astype(BF16)
+
+                    remote(
+                        mine, wgrad_place(name, dst, far, core), s + 5 + k, r + 2 * far + core,
+                        (target, z),
+                    ).start()
 
     def wgrad_finish(name, src, dst):
         s, r = sem_at["g_" + name]
@@ -749,20 +804,17 @@
 
             @pl.when(c == core)
             def _():
-                for q in range(4):
-                    for other_core in (0, 1):
-                        target = chip_target(q) + other_core
-                        here = wgrad_piece(name, src, target, core)
-                        if q or other_core != core:
-                            wait_send(here, s + 2 * q + other_core)
-                            wait_recv(
-                                wgrad_place(name, dst, target // 2, other_core), r + target
-                            )
-                        else:
-                            pltpu.make_async_copy(
-                                here, wgrad_place(name, dst, chip, core),
-                                lsem.at[len(WEIGHTS) + WEIGHTS.index(name)],
-                            ).wait()
+                here = wgrad_piece(name, src, d, core)
+                for i in range(7):
+                    wait_send(here, s + i)
+                wait_recv(wgrad_place(name, dst, 0, 1 - core), r + 1 - core)
+                for slot in (1, 2):
+                    for k in (0, 1):
+                        wait_recv(wgrad_place(name, dst, slot, k), r + 2 * slot + k)
+                pltpu.make_async_copy(
+                    here, wgrad_place(name, dst, 0, core),
+                    lsem.at[len(WEIGHTS) + WEIGHTS.index(name)],
+                ).wait()
 
     gather_x = Gather("ag_x", buf_a)
     gather_d = Gather("ag_d", buf_c)
@@ -773,13 +825,19 @@
     scatter_i = Scatter("rs_i", part, part_x, part_r)
     scatter_m = Scatter("rs_m", mix, mix_x, mix_r)
 
-    gather_x.start(x_in)
     sz, rz = sem_at["sm_z"]
     sd, rd = sem_at["sm_d"]
     small[d, z] = small_in[...]
     for i in range(1, sp):
         peer = (z + i) % sp
         remote(small_in, small.at[d, z], sz + i, rz + z, (d, peer)).start()
+    gather_x.start(x_in)
+    for i in range(1, sp):
+        peer = (z + i) % sp
+        wait_recv(small.at[d, peer], rz + peer)
+    for i in range(1, dp):
+        peer = (d + i) % dp
+        remote(small.at[d], small.at[d], sd + i, rd + d, (peer, z)).start()
     weight_send("qkv", wqkv_in, w_qkv)
     weight_send("out", wout_in, w_out)
 
@@ -799,12 +857,6 @@
         for ref in (w_gate, w_up, w_down):
             ref[:, plan.ff_slim :] = jnp.zeros((width, pad), BF16)
 
-    for i in range(1, sp):
-        peer = (z + i) % sp
-        wait_recv(small.at[d, peer], rz + peer)
-    for i in range(1, dp):
-        peer = (d + i) % dp
-        remote(small.at[d], small.at[d], sd + i, rd + d, (peer, z)).start()
     for i in range(1, dp):
         peer = (d + i) % dp
         wait_recv(small.at[peer], rd + peer)
@@ -832,6 +884,10 @@
         def _():
             gather_x.hop(i)
 
+        @pl.when(i == last - 1)
+        def _():
+            weight_forward("qkv", w_qkv)
+
         t = order(i)
         gather_x.need(t)
         src, dst = rows_of(buf_a, t), rows_of(n1, t)
@@ -846,8 +902,10 @@
     n1_copy = pltpu.make_async_copy(n1, n1_hbm, lsem.at[2 * len(WEIGHTS)])
     n1_copy.start()
 
+    weight_forward("out", w_out)
+    weight_send("gate", wg_in, w_gate)
+    weight_send("up", wu_in, w_up)
     weight_wait("qkv", wqkv_in, w_qkv)
-    weight_send("gate", wg_in, w_gate)
     low = iota((1, 128), 1) < 64
     first_half = iota((1, 128), 1) % 64 < ROT // 2
 
@@ -922,9 +980,9 @@
     gather_d.hop(1)
     gather_x.drain(x_in)
 
+    weight_forward("gate", w_gate)
+    weight_send("down", wd_in, w_down)
     weight_wait("out", wout_in, w_out)
-    weight_send("up", wu_in, w_up)
-    weight_send("down", wd_in, w_down)
 
     def far_first(i):
         return jnp.where(z < last - z, last - i, i)
@@ -942,9 +1000,11 @@
         scatter_o.core(t)
 
     scatter_o.step(0)
+    weight_forward("up", w_up)
     for k in range(1, sp - 1):
         scatter_o.step(k)
         gather_d.hop(k + 1)
+    weight_forward("down", w_down)
     scatter_o.final(acc)
 
     own_n = block(buf_a, z, c)
@@ -1009,16 +1069,18 @@
             dst[sl, :] = dot_tn(tokens[:, sl], cols[...]).astype(BF16)
 
     scatter_n.step(0)
-    weight_drain("down", wd_in)
+    weight_drain("down", wd_in, w_down)
+    weight_drain("gate", wg_in, w_gate)
+    weight_drain("up", wu_in, w_up)
     wgrad(buf_c, act, w_down)
-    wgrad_send("down", w_down, rg_down)
+    wgrad_send("down", w_down, rg_down, st_down)
     scatter_n.step(1)
     wgrad(buf_a, dgate, w_gate)
-    wgrad_send("gate", w_gate, rg_gate)
+    wgrad_send("gate", w_gate, rg_gate, st_gate)
     for k in range(2, sp - 1):
         scatter_n.step(k)
     wgrad(buf_a, dup, w_up)
-    wgrad_send("up", w_up, rg_up)
+    wgrad_send("up", w_up, rg_up, st_up)
     scatter_n.final(acc)
 
     gather_n.drain(own_n)
@@ -1046,8 +1108,11 @@
         own_b[sl, :] = back.astype(BF16)
 
     gather_b.start(own_b)
+    datt = dgate.at[:, pl.ds(0, plan.head_cols)]
+    dqkv = act.at[:, pl.ds(0, plan.qkv_cols)]
     scatter_n.drain()
     scatter_m.step(0)
+    wgrad_merge("down", w_down, rg_down, st_down)
 
     @pl.loop(0, sp)
     def _(i):
@@ -1062,6 +1127,8 @@
         t = order(i)
         gather_b.need(t)
         datt[tile(t, chunk), :] = dot_nt(rows_of(buf_b, t)[...], w_out[...]).astype(BF16)
+
+    wgrad_merge("gate", w_gate, rg_gate, st_gate)
 
     biassum[...] = jnp.zeros_like(biassum)
 
@@ -1117,6 +1184,8 @@
         for p in range(plan.pairs):
             attention_back(r, p)
 
+    wgrad_merge("up", w_up, rg_up, st_up)
+
     @pl.loop(0, sp)
     def _(i):
         t = far_first(i)
@@ -1130,9 +1199,11 @@
         scatter_i.core(t)
 
     scatter_i.step(0)
+    weight_drain("qkv", wqkv_in, w_qkv)
+    weight_drain("out", wout_in, w_out)
     n1_back.wait()
     wgrad(buf_a, dqkv, w_qkv)
-    wgrad_send("qkv", w_qkv, rg_qkv)
+    wgrad_send("qkv", w_qkv, rg_qkv, st_qkv)
     scatter_i.step(1)
 
     @pl.loop(0, width // 256)
@@ -1140,9 +1211,10 @@
         sl = tile(n, 256)
         w_out[:, sl] = dot_tn(att[...], buf_b[:, sl]).astype(BF16)
 
-    wgrad_send("out", w_out, rg_out)
+    wgrad_send("out", w_out, rg_out, st_out)
     for k in range(2, sp - 1):
         scatter_i.step(k)
+    wgrad_merge("qkv", w_qkv, rg_qkv, st_qkv)
     scatter_m.final(acc)
 
     @pl.loop(0, slots // 32)
@@ -1152,6 +1224,7 @@
         keep = jnp.where(pos < small_in[7:8, 0:1], 1.0, 0.0)
         out_ref[sl, :] = (keep * (resid[sl, :] + acc[sl, :])).astype(BF16)
 
+    wgrad_merge("out", w_out, rg_out, st_out)
     scatter_i.final(acc)
 
     @pl.loop(0, slots // 32)
@@ -1198,8 +1271,6 @@
         ("qkv", w_qkv, rg_qkv), ("out", w_out, rg_out),
     ):
         wgrad_finish(name, src, dst)
-    for name, src in (("qkv", wqkv_in), ("out", wout_in), ("gate", wg_in), ("up", wu_in)):
-        weight_drain(name, src)
     gather_d.drain(own_d)
     gather_b.drain(own_b)
     scatter_m.drain()
@@ -1238,7 +1309,7 @@
     sem_at = {}
     for name in WEIGHTS:
         sem_at["w_" + name] = plan.sems(8, dp)
-        sem_at["g_" + name] = plan.sems(8, dp)
+        sem_at["g_" + name] = plan.sems(7, 8)
     for name in ("ag_x", "ag_d", "ag_n", "ag_b"):
         sem_at[name] = plan.sems(2 + 2 * sp, 2 * sp)
     for name in ("rs_o", "rs_n", "rs_i", "rs_m"):
@@ -1269,11 +1340,11 @@
         jax.ShapeDtypeStruct((slots, width), BF16),
         jax.ShapeDtypeStruct((slots, width), F32),
         jax.ShapeDtypeStruct((8, plan.shard + 128), F32),
-        jax.ShapeDtypeStruct((plan.chips,) + qkv_weight.shape, BF16),
-        jax.ShapeDtypeStruct((plan.chips,) + out_weight.shape, BF16),
-        jax.ShapeDtypeStruct((plan.chips,) + gate_weight.shape, BF16),
-        jax.ShapeDtypeStruct((plan.chips,) + up_weight.shape, BF16),
-        jax.ShapeDtypeStruct((plan.chips,) + down_weight.shape, BF16),
+        jax.ShapeDtypeStruct((3,) + qkv_weight.shape, BF16),
+        jax.ShapeDtypeStruct((3,) + out_weight.shape, BF16),
+        jax.ShapeDtypeStruct((3,) + gate_weight.shape, BF16),
+        jax.ShapeDtypeStruct((3,) + up_weight.shape, BF16),
+        jax.ShapeDtypeStruct((3,) + down_weight.shape, BF16),
         jax.ShapeDtypeStruct((plan.tokens, width), BF16),
     ]
     tokens, heads, ff = plan.tokens, plan.head_cols, plan.ff_wide
@@ -1299,8 +1370,6 @@
         pltpu.VMEM((2, plan.pairs, plan.seq, 128), BF16),
         pltpu.VMEM((2, plan.pairs, plan.seq, 128), BF16),
         pltpu.VMEM((tokens, heads), BF16),
-        pltpu.VMEM((tokens, heads), BF16),
-        pltpu.VMEM((tokens, plan.qkv_cols), BF16),
         pltpu.VMEM((plan.chunk, plan.qkv_cols), F32),
         pltpu.VMEM((tokens, ff), BF16),
         pltpu.VMEM((tokens, ff), BF16),
@@ -1319,6 +1388,11 @@
         pltpu.VMEM((dp, 8, plan.shard + 128), F32),
         pltpu.VMEM((dp, 8, plan.shard + 128), F32),
         pltpu.VMEM((sp, 8, plan.shard + 128), F32),
+        pltpu.VMEM((2, plan.shard, plan.qkv_cols), BF16),
+        pltpu.VMEM((2, heads, plan.shard), BF16),
+        pltpu.VMEM((2, plan.shard, ff), BF16),
+        pltpu.VMEM((2, plan.shard, ff), BF16),
+        pltpu.VMEM((2, plan.shard, ff), BF16),
     ]
     outs = pl.pallas_call(
         functools.partial(layer_kernel, plan, sem_at),

time: 397 us -> 328 us (0.83)
  Pallas kernels: 379 us -> 312 us
    pallas_call x1, Pallas kernels: 379 us -> 312 us  [per_device_fast(): pl.pallas_call(functools.partial(layer_kernel, plan, sem_at), out_shape=o...]
where the time goes in v2:
time: 328 us
  Pallas kernels  312 us (95%)
  other arithmetic  10.9 us (3%)
  local copies, waits for them, and re-layouts  3.78 us (1%)
    pallas_call x1, Pallas kernels, per_device_fast(): pl.pallas_call(functools.partial(layer_kernel, plan, sem_at), out_shape=o...  312 us
    reduce_sum x4, other arithmetic, per_device_fast(): grads = [jnp.sum(g.astype(F32), axis=0) for g in outs[3:8]]  8.71 us

profile of v2, /device:TPU:0, one launch (start us, length us, event | category | flops | bytes accessed | tf_op | source)
XLA Modules:
  0.0 327.9 jit_solution(13868460277363392444)
XLA Ops:
  0.7 0.7 maximum_convert_fusion
  1.4 0.1 pad_select_fusion
  1.4 0.7 convert_element_type.25
  2.1 0.1 select_bitcast_fusion
  2.8 0.1 pad.6.clone
  2.9 0.7 maximum_maximum_fusion.refs_2_
  3.6 311.8 %shard_map.238 = (bf16[128,2048]{1,0:T(8,128)(2,1)}, f32[128,2048]{1,0:T(8,128)}, f32[8,384]{1,0:T(8,128)}, bf16[3,256,1536]{2,1,0:T(8,128)(2,1)}, bf16[3,512,25...) custom-call(bf16[128,2048]{1,0:T(8,128)(2,1)} %bitcast.23, ...), custom_call_target="tpu_custom_call" | custom-call | tf_op jit(solution)/shard_map/pallas_call | solution.py:1397
  315.4 0.0 copy-start
  315.4 4.9 %convert_reduce_fusion.1 = (f32[256,1408]{1,0:T(8,128)}, f32[256,1408]{1,0:T(8,128)}) fusion(bf16[3,256,1408]{2,1,0:T(8,128)(2,1)} %get-tuple-element.27, bf16[3,256,1408]{2,1,0:T(8,128)(2,1)} %get-tuple-element.26), kind=kLoop, calls=%fused_computation.1 | loop fusion | flops 3604480 | bytes 7208960 | tf_op jit(solution)/shard_map/reduce_sum | solution.py:1415
  320.3 0.0 copy-start.1
  320.3 0.0 copy-done
  320.3 1.5 convert_reduce_fusion
  321.8 0.0 copy-start.3
  321.8 0.7 copy-done.1
  322.5 0.0 copy-start.5
  322.5 0.0 copy-start.4
  322.5 0.0 copy-start.2
  322.5 1.4 convert_reduce_fusion.3
  323.9 0.0 copy-done.3
  323.9 0.9 convert_reduce_fusion.4
  324.8 0.0 copy-done.5
  324.9 0.1 constant_dynamic-slice_fusion
  324.9 0.5 slice_bitcast_fusion.1
  325.5 0.6 dynamic_slice.7
  326.1 0.0 copy-done.4
  326.1 0.8 copy.30
  326.9 0.0 copy-done.2
  326.9 1.0 copy.31
  (2 shorter events, 0.0 us)
Async XLA Ops:
  315.4 4.9 %copy-start = (bf16[3,256,1536]{2,1,0:T(8,128)(2,1)S(1)}, bf16[3,256,1536]{2,1,0:T(8,128)(2,1)}, u32[]{:S(2)}) copy-start(bf16[3,256,1536]{2,1,0:T(8,128)(2,1)} %get-tuple-element.23) | copy-start | bytes 7077892
  320.3 2.2 copy-start.1
  321.8 2.1 copy-start.3
  322.5 2.3 copy-start.5
  322.5 3.6 %copy-start.4 = (bf16[128,2048]{1,0:T(8,128)(2,1)S(1)}, bf16[128,2048]{1,0:T(8,128)(2,1)}, u32[]{:S(2)}) copy-start(bf16[128,2048]{1,0:T(8,128)(2,1)} %get-tuple-element.20) | copy-start | bytes 1572868
  322.5 4.4 %copy-start.2 = (f32[128,2048]{1,0:T(8,128)S(1)}, f32[128,2048]{1,0:T(8,128)}, u32[]{:S(2)}) copy-start(f32[128,2048]{1,0:T(8,128)} %get-tuple-element.21) | copy-start | bytes 3145732

commit v3 on v2

--- a/solution.py
+++ b/solution.py
@@ -449,8 +449,8 @@
         w_qkv, w_out, w_gate, w_up, w_down,
         buf_a, buf_b, buf_c,
         part, part_x, part_r, mix, mix_x, mix_r,
-        q_ref, k_ref, v_ref, att, raw,
-        act, dgate, dup, kacc, vacc,
+        q_ref, k_ref, v_ref, att,
+        act, dgate, dup,
         resid, acc, dres,
         small, vecs, qbias, lens, colsum, biassum, send_sum, recv_sum, z_sum,
         st_qkv, st_out, st_gate, st_up, st_down,
@@ -480,11 +480,24 @@
     def block(buf, t, core):
         return buf.at[pl.ds(pl.multiple_of(t * chunk + core * slots, slots), slots)]
 
+    def sub_block(buf, t, core, at):
+        start, size = at
+        return buf.at[pl.ds(pl.multiple_of(t * chunk + core * slots + start, size), size)]
+
     def rows_of(buf, t):
         return buf.at[tile(t, chunk)]
 
-    def slot_block(buf, t):
-        return buf.at[tile(t, slots)]
+    def spans(size, step):
+        return [slice(i, min(i + step, size)) for i in range(0, size, step)]
+
+    def slot_block(buf, t, at):
+        start, size = at
+        return buf.at[pl.ds(pl.multiple_of(t * slots + start, size), size)]
+
+    whole = (0, slots)
+    def parts(count):
+        return [(h * (slots // count), slots // count) for h in range(count)]
+
 
     barrier = pltpu.get_barrier_semaphore()
     for i in range(1, dp):
@@ -494,13 +507,13 @@
     pl.semaphore_wait(barrier, dp + sp - 2)
 
     class Gather:
-        def __init__(self, name, buf):
+        def __init__(self, name, buf, at=whole):
             self.s, self.r = sem_at[name]
-            self.buf = buf
+            self.buf, self.at = buf, at
 
         def start(self, own):
             s, r = self.s, self.r
-            dst = block(self.buf, z, c)
+            dst = sub_block(self.buf, z, c, self.at)
 
             @pl.when(z < last)
             def _():
@@ -517,7 +530,7 @@
             for sign in (-1, 1):
                 t = z + sign * k
                 nxt = z - sign
-                blk = block(self.buf, t, c)
+                blk = sub_block(self.buf, t, c, self.at)
 
                 @pl.when((t >= 0) & (t <= last))
                 def _():
@@ -530,7 +543,7 @@
                     remote(blk, blk, s + 2 + sp + t, r + sp + t, sib).start()
 
         def need(self, t):
-            wait_recv(block(self.buf, t, oc), self.r + sp + t)
+            wait_recv(sub_block(self.buf, t, oc, self.at), self.r + sp + t)
 
         def drain(self, own):
             s = self.s
@@ -558,27 +571,27 @@
         return jnp.where(i <= 2 * low, paired, single)
 
     def add_into(dst, terms):
-        @pl.loop(0, slots // 32)
+        @pl.loop(0, dst.shape[0] // ADD_ROWS)
         def _(i):
-            sl = tile(i, 32)
+            sl = tile(i, ADD_ROWS)
             total = dst[sl, :].astype(F32)
             for term in terms:
                 total = total + term[sl, :].astype(F32)
             dst[sl, :] = total.astype(dst.dtype)
 
     class Scatter:
-        def __init__(self, name, parts, from_core, from_line):
+        def __init__(self, name, parts, from_core, from_line, at=whole):
             self.s, self.r = sem_at[name]
-            self.p, self.x, self.l = parts, from_core, from_line
+            self.p, self.x, self.l, self.at = parts, from_core, from_line, at
 
         def core(self, t):
             remote(
-                block(self.p, t, oc), slot_block(self.x, t), self.s + t, self.r + t, sib
+                sub_block(self.p, t, oc, self.at), slot_block(self.x, t, self.at), self.s + t, self.r + t, sib
             ).start()
 
         def send(self, t, from_end, nbr, slot):
-            mine = block(self.p, t, c)
-            xs = slot_block(self.x, t)
+            mine = sub_block(self.p, t, c, self.at)
+            xs = slot_block(self.x, t, self.at)
             wait_recv(xs, self.r + t)
 
             @pl.when(from_end)
@@ -587,12 +600,12 @@
 
             @pl.when(jnp.logical_not(from_end))
             def _():
-                ls = slot_block(self.l, t)
+                ls = slot_block(self.l, t, self.at)
                 wait_recv(ls, self.r + sp + t)
                 add_into(mine, [xs, ls])
 
             remote(
-                mine, slot_block(self.l, slot), self.s + sp + t, self.r + sp + slot, (d, nbr)
+                mine, slot_block(self.l, slot, self.at), self.s + sp + t, self.r + sp + slot, (d, nbr)
             ).start()
 
         def step(self, n):
@@ -610,34 +623,35 @@
                 self.send(t, z == 0, z + 1, jnp.where(t == z + 1, sp, t))
 
         def final(self, total):
-            mine = block(self.p, z, c)
-            xs = slot_block(self.x, z)
+            total = total.at[pl.ds(*self.at)]
+            mine = sub_block(self.p, z, c, self.at)
+            xs = slot_block(self.x, z, self.at)
             wait_recv(xs, self.r + z)
 
-            @pl.loop(0, slots // 32)
+            @pl.loop(0, self.at[1] // ADD_ROWS)
             def _(i):
-                sl = tile(i, 32)
+                sl = tile(i, ADD_ROWS)
                 total[sl, :] = mine[sl, :].astype(F32) + xs[sl, :].astype(F32)
 
             @pl.when(z < last)
             def _():
-                ls = slot_block(self.l, z)
+                ls = slot_block(self.l, z, self.at)
                 wait_recv(ls, self.r + sp + z)
                 add_into(total, [ls])
 
             @pl.when(z > 0)
             def _():
-                ls = slot_block(self.l, sp)
+                ls = slot_block(self.l, sp, self.at)
                 wait_recv(ls, self.r + sp + sp)
                 add_into(total, [ls])
 
         def drain(self):
             for t in range(sp):
-                wait_send(slot_block(self.x, t), self.s + t)
+                wait_send(slot_block(self.x, t, self.at), self.s + t)
 
                 @pl.when(t != z)
                 def _():
-                    wait_send(slot_block(self.x, t), self.s + sp + t)
+                    wait_send(slot_block(self.x, t, self.at), self.s + sp + t)
 
     def chip_target(q):
         cx, cy = chip % 2, chip // 2
@@ -818,11 +832,11 @@
 
     gather_x = Gather("ag_x", buf_a)
     gather_d = Gather("ag_d", buf_c)
-    gather_n = Gather("ag_n", buf_a)
-    gather_b = Gather("ag_b", buf_b)
-    scatter_o = Scatter("rs_o", part, part_x, part_r)
-    scatter_n = Scatter("rs_n", part, part_x, part_r)
-    scatter_i = Scatter("rs_i", part, part_x, part_r)
+    gather_n = [Gather("ag_n%d" % h, buf_a, at) for h, at in enumerate(parts(PARTS_FORWARD))]
+    gather_b = [Gather("ag_b%d" % h, buf_b, at) for h, at in enumerate(parts(PARTS_BACK))]
+    scatter_o = [Scatter("rs_o%d" % h, part, part_x, part_r, at) for h, at in enumerate(parts(PARTS_FORWARD))]
+    scatter_n = [Scatter("rs_n%d" % h, part, part_x, part_r, at) for h, at in enumerate(parts(PARTS_BACK))]
+    scatter_i = [Scatter("rs_i%d" % h, part, part_x, part_r, at) for h, at in enumerate(parts(PARTS_LAST))]
     scatter_m = Scatter("rs_m", mix, mix_x, mix_r)
 
     sz, rz = sem_at["sm_z"]
@@ -839,7 +853,6 @@
         peer = (d + i) % dp
         remote(small.at[d], small.at[d], sd + i, rd + d, (peer, z)).start()
     weight_send("qkv", wqkv_in, w_qkv)
-    weight_send("out", wout_in, w_out)
 
     block(buf_a, z, c)[...] = x_in[...]
     own_len = small_in[7:8, 0:1]
@@ -880,21 +893,28 @@
 
     @pl.loop(0, sp)
     def _(i):
+        @pl.when(i == last - 1)
+        def _():
+            weight_forward("qkv", w_qkv)
+            weight_send("out", wout_in, w_out)
+
+        @pl.when(i == last)
+        def _():
+            weight_forward("out", w_out)
+            weight_send("gate", wg_in, w_gate)
+            weight_send("up", wu_in, w_up)
+
         @pl.when(i > 0)
         def _():
             gather_x.hop(i)
 
-        @pl.when(i == last - 1)
-        def _():
-            weight_forward("qkv", w_qkv)
-
         t = order(i)
         gather_x.need(t)
         src, dst = rows_of(buf_a, t), rows_of(n1, t)
 
-        @pl.loop(0, chunk // 32)
+        @pl.loop(0, chunk // 64)
         def _(j):
-            sl = tile(j, 32)
+            sl = tile(j, 64)
             unit, _ = normalize(src[sl, :].astype(F32))
             dst[sl, :] = (unit * vecs[0:1, :] + vecs[1:2, :]).astype(BF16)
 
@@ -902,9 +922,6 @@
     n1_copy = pltpu.make_async_copy(n1, n1_hbm, lsem.at[2 * len(WEIGHTS)])
     n1_copy.start()
 
-    weight_forward("out", w_out)
-    weight_send("gate", wg_in, w_gate)
-    weight_send("up", wu_in, w_up)
     weight_wait("qkv", wqkv_in, w_qkv)
     low = iota((1, 128), 1) < 64
     first_half = iota((1, 128), 1) % 64 < ROT // 2
@@ -915,23 +932,23 @@
         )
         return v * cosine + swapped * sine
 
+    raw = (resid, dres)
+
     @pl.loop(0, sp)
     def _(t):
         src = rows_of(n1, t)
 
-        @pl.loop(0, plan.qkv_cols // 256)
-        def _(n):
-            sl = tile(n, 256)
-            raw[:, sl] = dot_nn(src[...], w_qkv[:, sl]) + qbias[0:1, sl]
+        both = dot_nn(src[...], w_qkv[...]) + qbias[0:1, :]
+        for r in range(2):
+            raw[r][:, 0 : plan.qkv_cols] = both[r * slots : (r + 1) * slots]
 
         here = tile(t, slots)
         cosine, sine = cos_in[here, :], sin_in[here, :]
         for r in range(2):
-            rs = slice(r * slots, (r + 1) * slots)
             for p in range(plan.pairs):
-                v0 = raw[rs, p * 384 : p * 384 + 128]
-                v1 = raw[rs, p * 384 + 128 : p * 384 + 256]
-                v2 = raw[rs, p * 384 + 256 : p * 384 + 384]
+                v0 = raw[r][:, p * 384 : p * 384 + 128]
+                v1 = raw[r][:, p * 384 + 128 : p * 384 + 256]
+                v2 = raw[r][:, p * 384 + 256 : p * 384 + 384]
                 r0 = rotated(v0, cosine, sine)
                 r1 = rotated(v1, cosine, sine)
                 r2 = rotated(v2, cosine, sine)
@@ -992,100 +1009,134 @@
         t = far_first(i)
         src, dst = rows_of(att, t), rows_of(part, t)
 
-        @pl.loop(0, width // 256)
-        def _(n):
-            sl = tile(n, 256)
+        for sl in spans(width, 512):
             dst[:, sl] = dot_nn(src[...], w_out[:, sl]).astype(BF16)
 
-        scatter_o.core(t)
-
-    scatter_o.step(0)
-    weight_forward("up", w_up)
-    for k in range(1, sp - 1):
-        scatter_o.step(k)
-        gather_d.hop(k + 1)
-    weight_forward("down", w_down)
-    scatter_o.final(acc)
+        for part_o in scatter_o:
+            part_o.core(t)
 
     own_n = block(buf_a, z, c)
 
-    @pl.loop(0, slots // 32)
-    def _(i):
-        sl = tile(i, 32)
-        hidden = x_in[sl, :].astype(F32) + acc[sl, :]
-        resid[sl, :] = hidden
-        unit, _ = normalize(hidden)
-        own_n[sl, :] = (unit * vecs[2:3, :] + vecs[3:4, :]).astype(BF16)
-
-    gather_n.start(own_n)
-    for i in range(sp):
-        gather_d.need(i)
-    scatter_o.drain()
+    def second_norm(at):
+        rows = pl.ds(*at)
+        x_rows, acc_rows, resid_rows, n_rows = (
+            ref.at[rows] for ref in (x_in, acc, resid, own_n)
+        )
+
+        @pl.loop(0, at[1] // 32)
+        def _(i):
+            sl = tile(i, 32)
+            hidden = x_rows[sl, :].astype(F32) + acc_rows[sl, :]
+            resid_rows[sl, :] = hidden
+            unit, _ = normalize(hidden)
+            n_rows[sl, :] = (unit * vecs[2:3, :] + vecs[3:4, :]).astype(BF16)
+
+    def pipeline(scatters, total, middle, gathers, buf, extra):
+        scatters[0].step(0)
+        for h, scatter in enumerate(scatters):
+            for k in range(1, sp - 1):
+                extra()
+                scatter.step(k)
+                if h:
+                    gathers[h - 1].hop(k)
+            if h + 1 < len(scatters):
+                scatters[h + 1].step(0)
+            extra()
+            scatter.final(total)
+            middle(scatter.at)
+            gathers[h].start(sub_block(buf, z, c, scatter.at))
+            if h:
+                for k in range(sp - 1, sp):
+                    gathers[h - 1].hop(k)
+
+    def one_by_one(*steps):
+        todo = list(steps)
+
+        def extra():
+            if todo:
+                todo.pop(0)()
+
+        return extra, todo
+
+    extra, todo = one_by_one(
+        lambda: None,
+        lambda: (weight_forward("up", w_up), gather_d.hop(2)),
+        lambda: None,
+        lambda: weight_forward("down", w_down),
+    )
+    pipeline(scatter_o, acc, second_norm, gather_n, buf_a, extra)
+    for step in todo:
+        step()
+    for part_o in scatter_o:
+        part_o.drain()
     n1_copy.wait()
+
+    def feed_forward(t):
+        for part_n in gather_n:
+            part_n.need(t)
+        tok = rows_of(buf_a, t)
+        act_t, dg_t, du_t = rows_of(act, t), rows_of(dgate, t), rows_of(dup, t)
+        for sl in spans(plan.ff_wide, 256):
+            gate = dot_nn(tok[...], w_gate[:, sl])
+            up = dot_nn(tok[...], w_up[:, sl])
+            sig = jax.nn.sigmoid(gate)
+            silu = gate * sig
+            act_t[:, sl] = (silu * up).astype(BF16)
+            du_t[:, sl] = silu.astype(BF16)
+            dg_t[:, sl] = (up * sig * (1.0 + gate * (1.0 - sig))).astype(BF16)
+
+    def feed_back(t):
+        gather_d.need(t)
+        dg_t, du_t = rows_of(dgate, t), rows_of(dup, t)
+        gout, part_t = rows_of(buf_c, t), rows_of(part, t)
+        for sl in spans(plan.ff_wide, 256):
+            d_act = dot_nn(gout[...], w_down[:, sl])
+            du_t[:, sl] = (d_act * du_t[:, sl].astype(F32)).astype(BF16)
+            dg_t[:, sl] = (d_act * dg_t[:, sl].astype(F32)).astype(BF16)
+        for sl in spans(width, 512):
+            part_t[:, sl] = (
+                dot_nt(dg_t[...], w_gate[sl, :]) + dot_nt(du_t[...], w_up[sl, :])
+            ).astype(BF16)
+        for part_n in scatter_n:
+            part_n.core(t)
 
     weight_wait("gate", wg_in, w_gate)
     weight_wait("up", wu_in, w_up)
-    weight_wait("down", wd_in, w_down)
 
     @pl.loop(0, sp)
     def _(i):
         @pl.when(i > 0)
         def _():
-            gather_n.hop(i)
-
-        t = order(i)
-        gather_n.need(t)
-        tok, gout = rows_of(buf_a, t), rows_of(buf_c, t)
-        act_t, dg_t, du_t = rows_of(act, t), rows_of(dgate, t), rows_of(dup, t)
-        part_t, mix_t = rows_of(part, t), rows_of(mix, t)
-
-        @pl.loop(0, plan.ff_wide // 256)
+            gather_n[-1].hop(i)
+
+        @pl.when(i == last)
+        def _():
+            for k in range(3, sp):
+                gather_d.hop(k)
+
+        feed_forward(order(i))
+
+        @pl.when(i == BACK_FROM)
+        def _():
+            weight_wait("down", wd_in, w_down)
+
+        first = jnp.where(i == BACK_FROM, 0, i)
+        stop = jnp.where(i < BACK_FROM, 0, i + 1)
+
+        @pl.loop(first, stop)
+        def _(j):
+            feed_back(order(j))
+
+    def wgrad(tokens, cols, dst, start, stop):
+        @pl.loop(start, stop)
         def _(n):
-            sl = tile(n, 256)
-            gate = dot_nn(tok[...], w_gate[:, sl])
-            up = dot_nn(tok[...], w_up[:, sl])
-            d_act = dot_nn(gout[...], w_down[:, sl])
-            sig = jax.nn.sigmoid(gate)
-            silu = gate * sig
-            act_t[:, sl] = (silu * up).astype(BF16)
-            du_t[:, sl] = (d_act * silu).astype(BF16)
-            dg_t[:, sl] = (d_act * up * sig * (1.0 + gate * (1.0 - sig))).astype(BF16)
-
-        @pl.loop(0, width // 256)
-        def _(n):
-            sl = tile(n, 256)
-            part_t[:, sl] = (
-                dot_nt(dg_t[...], w_gate[sl, :]) + dot_nt(du_t[...], w_up[sl, :])
-            ).astype(BF16)
-            mix_t[:, sl] = dot_nt(act_t[...], w_down[sl, :]).astype(BF16)
-
-        scatter_n.core(t)
-        scatter_m.core(t)
-
-    def wgrad(tokens, cols, dst):
-        @pl.loop(0, width // 256)
-        def _(n):
-            sl = tile(n, 256)
+            sl = tile(n, 512)
             dst[sl, :] = dot_tn(tokens[:, sl], cols[...]).astype(BF16)
 
-    scatter_n.step(0)
-    weight_drain("down", wd_in, w_down)
-    weight_drain("gate", wg_in, w_gate)
-    weight_drain("up", wu_in, w_up)
-    wgrad(buf_c, act, w_down)
-    wgrad_send("down", w_down, rg_down, st_down)
-    scatter_n.step(1)
-    wgrad(buf_a, dgate, w_gate)
-    wgrad_send("gate", w_gate, rg_gate, st_gate)
-    for k in range(2, sp - 1):
-        scatter_n.step(k)
-    wgrad(buf_a, dup, w_up)
-    wgrad_send("up", w_up, rg_up, st_up)
-    scatter_n.final(acc)
-
-    gather_n.drain(own_n)
-    n1_back = pltpu.make_async_copy(n1_hbm, buf_a, lsem.at[2 * len(WEIGHTS) + 1])
-    n1_back.start()
+    n_tiles = width // 512
+    half = n_tiles // 2
+    for name, src, dst in (("down", wd_in, w_down), ("gate", wg_in, w_gate), ("up", wu_in, w_up)):
+        weight_drain(name, src, dst)
     colsum[...] = jnp.zeros_like(colsum)
     own_d, own_b = block(buf_c, z, c), block(buf_b, z, c)
 
@@ -1100,17 +1151,61 @@
             - unit * jnp.mean(scaled * unit, axis=-1, keepdims=True)
         )
 
-    @pl.loop(0, slots // 32)
-    def _(i):
-        sl = tile(i, 32)
-        back = own_d[sl, :].astype(F32) + norm_back(acc[sl, :], resid[sl, :], vecs[2:3, :], 2)
-        dres[sl, :] = back
-        own_b[sl, :] = back.astype(BF16)
-
-    gather_b.start(own_b)
+    def second_norm_back(at):
+        rows = pl.ds(*at)
+        d_rows, acc_rows, resid_rows, dres_rows, b_rows = (
+            ref.at[rows] for ref in (own_d, acc, resid, dres, own_b)
+        )
+
+        @pl.loop(0, at[1] // 32)
+        def _(i):
+            sl = tile(i, 32)
+            back = d_rows[sl, :].astype(F32) + norm_back(
+                acc_rows[sl, :], resid_rows[sl, :], vecs[2:3, :], 2
+            )
+            dres_rows[sl, :] = back
+            b_rows[sl, :] = back.astype(BF16)
+
+    def mixed():
+        @pl.loop(0, sp)
+        def _(i):
+            t = far_first(i)
+            act_t, mix_t = rows_of(act, t), rows_of(mix, t)
+            for sl in spans(width, 512):
+                mix_t[:, sl] = dot_nt(act_t[...], w_down[sl, :]).astype(BF16)
+            scatter_m.core(t)
+
+    def all_down():
+        wgrad(buf_c, act, w_down, 0, n_tiles)
+        wgrad_send("down", w_down, rg_down, st_down)
+
+    def first_gate():
+        wgrad(buf_a, dgate, w_gate, 0, half)
+
+    def last_gate():
+        wgrad(buf_a, dgate, w_gate, half, n_tiles)
+        wgrad_send("gate", w_gate, rg_gate, st_gate)
+
+    def first_up():
+        wgrad(buf_a, dup, w_up, 0, half)
+
+    def last_up():
+        wgrad(buf_a, dup, w_up, half, n_tiles)
+        wgrad_send("up", w_up, rg_up, st_up)
+
+    extra, todo = one_by_one(lambda: (mixed(), all_down()), first_gate, last_gate, first_up, last_up)
+    pipeline(scatter_n, acc, second_norm_back, gather_b, buf_b, extra)
+    for step in todo:
+        step()
+
+    for h, part_n in enumerate(gather_n):
+        part_n.drain(sub_block(buf_a, z, c, part_n.at))
+    n1_back = pltpu.make_async_copy(n1_hbm, buf_a, lsem.at[2 * len(WEIGHTS) + 1])
+    n1_back.start()
     datt = dgate.at[:, pl.ds(0, plan.head_cols)]
     dqkv = act.at[:, pl.ds(0, plan.qkv_cols)]
-    scatter_n.drain()
+    for part_n in scatter_n:
+        part_n.drain()
     scatter_m.step(0)
     wgrad_merge("down", w_down, rg_down, st_down)
 
@@ -1118,14 +1213,15 @@
     def _(i):
         @pl.when(i > 0)
         def _():
-            gather_b.hop(i)
+            gather_b[-1].hop(i)
 
         @pl.when((i > 0) & (i < last))
         def _():
             scatter_m.step(i)
 
         t = order(i)
-        gather_b.need(t)
+        for part_b in gather_b:
+            part_b.need(t)
         datt[tile(t, chunk), :] = dot_nt(rows_of(buf_b, t)[...], w_out[...]).astype(BF16)
 
     wgrad_merge("gate", w_gate, rg_gate, st_gate)
@@ -1153,21 +1249,20 @@
             dq_both = (jnp.where(low, dq[0], dq[1]) * scale).astype(BF16)
             dk_both = jnp.where(low, dk[0], dk[1])
             dv_both = jnp.where(low, dv[0], dv[1])
-            if qb == 0:
-                kacc[0:keys_to, :] = dk_both
-                vacc[0:keys_to, :] = dv_both
-            else:
-                kept = keys_to - q_rows
-                kacc[0:kept, :] += dk_both[0:kept]
-                vacc[0:kept, :] += dv_both[0:kept]
-                kacc[kept:keys_to, :] = dk_both[kept:keys_to]
-                vacc[kept:keys_to, :] = dv_both[kept:keys_to]
+            for t in range(keys_to // slots):
+                ts = slice(t * slots, (t + 1) * slots)
+                for at, new in ((t, dk_both), (sp + t, dv_both)):
+                    lanes = slice(at * 128, (at + 1) * 128)
+                    if t * slots < qb * q_rows:
+                        acc[:, lanes] += new[ts]
+                    else:
+                        acc[:, lanes] = new[ts]
             q_ref[r, p, qb * q_rows : keys_to, :] = dq_both
         for t in range(sp):
             ts = slice(t * slots, (t + 1) * slots)
             dqv = q_ref[r, p, ts, :].astype(F32)
-            dkv = (kacc[ts, :] * scale).astype(BF16).astype(F32)
-            dvv = vacc[ts, :].astype(BF16).astype(F32)
+            dkv = (acc[:, t * 128 : (t + 1) * 128] * scale).astype(BF16).astype(F32)
+            dvv = acc[:, (sp + t) * 128 : (sp + t + 1) * 128].astype(BF16).astype(F32)
             swapped = pltpu.roll(dkv, 64, 1)
             cosine, sine = cos_in[ts, :], -sin_in[ts, :]
             g0 = rotated(jnp.where(low, dqv, swapped), cosine, sine)
@@ -1191,29 +1286,31 @@
         t = far_first(i)
         dst, src = rows_of(part, t), rows_of(dqkv, t)
 
-        @pl.loop(0, width // 256)
-        def _(n):
-            sl = tile(n, 256)
+        for sl in spans(width, 512):
             dst[:, sl] = dot_nt(src[...], w_qkv[sl, :]).astype(BF16)
 
-        scatter_i.core(t)
-
-    scatter_i.step(0)
+        for part_i in scatter_i:
+            part_i.core(t)
+
+    for part_i in scatter_i:
+        part_i.step(0)
     weight_drain("qkv", wqkv_in, w_qkv)
     weight_drain("out", wout_in, w_out)
     n1_back.wait()
-    wgrad(buf_a, dqkv, w_qkv)
+    wgrad(buf_a, dqkv, w_qkv, 0, n_tiles)
     wgrad_send("qkv", w_qkv, rg_qkv, st_qkv)
-    scatter_i.step(1)
-
-    @pl.loop(0, width // 256)
+    for part_i in scatter_i:
+        part_i.step(1)
+
+    @pl.loop(0, width // 1024)
     def _(n):
-        sl = tile(n, 256)
+        sl = tile(n, 1024)
         w_out[:, sl] = dot_tn(att[...], buf_b[:, sl]).astype(BF16)
 
     wgrad_send("out", w_out, rg_out, st_out)
     for k in range(2, sp - 1):
-        scatter_i.step(k)
+        for part_i in scatter_i:
+            part_i.step(k)
     wgrad_merge("qkv", w_qkv, rg_qkv, st_qkv)
     scatter_m.final(acc)
 
@@ -1225,13 +1322,15 @@
         out_ref[sl, :] = (keep * (resid[sl, :] + acc[sl, :])).astype(BF16)
 
     wgrad_merge("out", w_out, rg_out, st_out)
-    scatter_i.final(acc)
-
-    @pl.loop(0, slots // 32)
-    def _(i):
-        sl = tile(i, 32)
-        back = norm_back(acc[sl, :], x_in[sl, :].astype(F32), vecs[0:1, :], 0)
-        grad_ref[sl, :] = dres[sl, :] + back
+    for part_i in scatter_i:
+        part_i.final(acc)
+        first = part_i.at[0] // 32
+
+        @pl.loop(first, first + part_i.at[1] // 32)
+        def _(i):
+            sl = tile(i, 32)
+            back = norm_back(acc[sl, :], x_in[sl, :].astype(F32), vecs[0:1, :], 0)
+            grad_ref[sl, :] = dres[sl, :] + back
 
     per = plan.shard
     for i in range(dp):
@@ -1272,9 +1371,11 @@
     ):
         wgrad_finish(name, src, dst)
     gather_d.drain(own_d)
-    gather_b.drain(own_b)
+    for h, part_b in enumerate(gather_b):
+        part_b.drain(sub_block(buf_b, z, c, part_b.at))
     scatter_m.drain()
-    scatter_i.drain()
+    for part_i in scatter_i:
+        part_i.drain()
     for i in range(1, sp):
         wait_send(small_in, sz + i)
         wait_send(z_sum.at[z], sb + i)
@@ -1283,6 +1384,11 @@
         wait_send(send_sum.at[0], sa + i)
 
 
+PARTS_FORWARD = 1
+PARTS_BACK = 1
+PARTS_LAST = 1
+BACK_FROM = 1
+ADD_ROWS = 64
 WEIGHTS = ("qkv", "out", "gate", "up", "down")
 
 
@@ -1296,6 +1402,36 @@
     cos_head[:, :half], cos_head[:, half:ROT] = cosine, cosine
     sin_head[:, :half], sin_head[:, half:ROT] = -sine, sine
     return np.tile(cos_head, (1, 2)), np.tile(sin_head, (1, 2))
+
+
+def last_sums_kernel(*refs):
+    count = len(refs) // 2
+    for src, dst in zip(refs[:2], refs[count : count + 2]):
+        dst[...] = src[...]
+    for src, dst in zip(refs[2:count], refs[count + 2 :]):
+        total = src[0].astype(F32)
+        for k in range(1, src.shape[0]):
+            total = total + src[k].astype(F32)
+        dst[...] = total
+
+
+def last_sums(*arrays):
+    steps = 8
+    in_specs, out_specs, out_shape = [], [], []
+    for i, array in enumerate(arrays):
+        rows, cols = array.shape[-2:]
+        block = (rows // steps, cols)
+        out_specs.append(pl.BlockSpec(block, lambda j: (j, 0)))
+        if i < 2:
+            in_specs.append(pl.BlockSpec(block, lambda j: (j, 0)))
+            out_shape.append(jax.ShapeDtypeStruct((rows, cols), array.dtype))
+        else:
+            in_specs.append(pl.BlockSpec((array.shape[0],) + block, lambda j: (0, j, 0)))
+            out_shape.append(jax.ShapeDtypeStruct((rows, cols), F32))
+    return pl.pallas_call(
+        last_sums_kernel, grid=(steps,), in_specs=in_specs, out_specs=out_specs,
+        out_shape=out_shape,
+    )(*arrays)
 
 
 def per_device_fast(
@@ -1310,9 +1446,11 @@
     for name in WEIGHTS:
         sem_at["w_" + name] = plan.sems(8, dp)
         sem_at["g_" + name] = plan.sems(7, 8)
-    for name in ("ag_x", "ag_d", "ag_n", "ag_b"):
+    split = (("o", PARTS_FORWARD), ("n", PARTS_BACK), ("i", PARTS_LAST))
+    gathers = (("n", PARTS_FORWARD), ("b", PARTS_BACK))
+    for name in ["ag_x", "ag_d"] + ["ag_%s%d" % (n, h) for n, k in gathers for h in range(k)]:
         sem_at[name] = plan.sems(2 + 2 * sp, 2 * sp)
-    for name in ("rs_o", "rs_n", "rs_i", "rs_m"):
+    for name in ["rs_m"] + ["rs_%s%d" % (n, h) for n, k in split for h in range(k)]:
         sem_at[name] = plan.sems(2 * sp, 2 * sp + 1)
     for name in ("sm_z", "su_z"):
         sem_at[name] = plan.sems(sp, sp)
@@ -1370,12 +1508,9 @@
         pltpu.VMEM((2, plan.pairs, plan.seq, 128), BF16),
         pltpu.VMEM((2, plan.pairs, plan.seq, 128), BF16),
         pltpu.VMEM((tokens, heads), BF16),
-        pltpu.VMEM((plan.chunk, plan.qkv_cols), F32),
         pltpu.VMEM((tokens, ff), BF16),
         pltpu.VMEM((tokens, ff), BF16),
         pltpu.VMEM((tokens, ff), BF16),
-        pltpu.VMEM((plan.seq, 128), F32),
-        pltpu.VMEM((plan.seq, 128), F32),
         pltpu.VMEM((slots, width), F32),
         pltpu.VMEM((slots, width), F32),
         pltpu.VMEM((slots, width), F32),
@@ -1412,10 +1547,10 @@
     bias_grad = lax.dynamic_slice_in_dim(
         sums[:, plan.shard :].reshape(-1), z * qkv_bias.shape[0], qkv_bias.shape[0]
     )
-    grads = [jnp.sum(g.astype(F32), axis=0) for g in outs[3:8]]
+    done = last_sums(outs[0], outs[1], *outs[3:8])
     return (
-        outs[0][None], outs[1][None], own[0], own[1], own[2], own[3],
-        grads[0], bias_grad, grads[1], grads[2], grads[3], grads[4],
+        done[0][None], done[1][None], own[0], own[1], own[2], own[3],
+        done[2], bias_grad, done[3], done[4], done[5], done[6],
     )
 
 

time: 328 us -> 302 us (0.921)
  Pallas kernels: 312 us -> 297 us
  other arithmetic: 10.9 us -> 2.19 us
    pallas_call x1, Pallas kernels: 312 us -> 288 us  [per_device_fast(): pl.pallas_call(functools.partial(layer_kernel, plan, sem_at), out_shape=o...]
    pallas_call x0 -> x1, Pallas kernels: none -> 9.26 us  [last_sums(): pl.pallas_call(last_sums_kernel, grid=(steps,), in_specs=in_specs, out_sp...]
    reduce_sum x4 -> x0, other arithmetic: 8.71 us -> none  [per_device_fast(): grads = [jnp.sum(g.astype(F32), axis=0) for g in outs[3:8]]]
where the time goes in v3:
time: 302 us
  Pallas kernels  297 us (98%)
    pallas_call x1, Pallas kernels, per_device_fast(): pl.pallas_call(functools.partial(layer_kernel, plan, sem_at), out_shape=o...  288 us
    pallas_call x1, Pallas kernels, last_sums(): pl.pallas_call(last_sums_kernel, grid=(steps,), in_specs=in_specs, out_sp...  9.26 us

profile of v3, /device:TPU:0, one launch (start us, length us, event | category | flops | bytes accessed | tf_op | source)
XLA Modules:
  0.0 301.7 jit_solution(9439470838125797333)
XLA Ops:
  0.7 0.7 maximum_convert_fusion
  1.4 0.1 pad_select_fusion
  1.4 0.7 convert_element_type.10
  2.1 0.1 select_bitcast_fusion
  2.8 0.1 pad.6.clone
  2.9 0.7 maximum_maximum_fusion.refs_2_
  3.6 287.6 %shard_map.238 = (bf16[128,2048]{1,0:T(8,128)(2,1)}, f32[128,2048]{1,0:T(8,128)}, f32[8,384]{1,0:T(8,128)}, bf16[3,256,1536]{2,1,0:T(8,128)(2,1)}, bf16[3,512,25...) custom-call(bf16[128,2048]{1,0:T(8,128)(2,1)} %bitcast.21, ...), custom_call_target="tpu_custom_call" | custom-call | tf_op jit(solution)/shard_map/pallas_call | solution.py:1532
  291.1 0.0 copy-start
  291.1 9.3 %shard_map.239 = (bf16[128,2048]{1,0:T(8,128)(2,1)}, f32[128,2048]{1,0:T(8,128)}, f32[256,1536]{1,0:T(8,128)}, f32[512,256]{1,0:T(8,128)}, f32[256,1408]{1,0:T(8...) custom-call(bf16[128,2048]{1,0:T(8,128)(2,1)} %get-tuple-element.27.refs_0_, f32[128,2048]{1,0:T(8,128)} %get-tuple-element.28.refs_1_, ...), custom_call_target="tpu_custom_call" | custom-call | tf_op jit(solution)/shard_map/pallas_call | solution.py:1431
  300.4 0.0 copy-done
  300.4 0.1 constant_dynamic-slice_fusion
  300.5 0.5 slice_bitcast_fusion.1
  301.0 0.6 dynamic_slice.7
  (2 shorter events, 0.0 us)
Async XLA Ops:
  291.1 9.3 %copy-start = (f32[8,384]{1,0:T(8,128)S(1)}, f32[8,384]{1,0:T(8,128)}, u32[]{:S(2)}) copy-start(f32[8,384]{1,0:T(8,128)} %get-tuple-element.36) | copy-start | bytes 36868

commit v4 on v3

--- a/solution.py
+++ b/solution.py
@@ -1015,6 +1015,10 @@
         for part_o in scatter_o:
             part_o.core(t)
 
+        @pl.when(i == 1)
+        def _():
+            scatter_o[0].step(0)
+
     own_n = block(buf_a, z, c)
 
     def second_norm(at):
@@ -1031,8 +1035,9 @@
             unit, _ = normalize(hidden)
             n_rows[sl, :] = (unit * vecs[2:3, :] + vecs[3:4, :]).astype(BF16)
 
-    def pipeline(scatters, total, middle, gathers, buf, extra):
-        scatters[0].step(0)
+    def pipeline(scatters, total, middle, gathers, buf, extra, started=False):
+        if not started:
+            scatters[0].step(0)
         for h, scatter in enumerate(scatters):
             for k in range(1, sp - 1):
                 extra()
@@ -1064,7 +1069,7 @@
         lambda: None,
         lambda: weight_forward("down", w_down),
     )
-    pipeline(scatter_o, acc, second_norm, gather_n, buf_a, extra)
+    pipeline(scatter_o, acc, second_norm, gather_n, buf_a, extra, True)
     for step in todo:
         step()
     for part_o in scatter_o:
@@ -1292,8 +1297,11 @@
         for part_i in scatter_i:
             part_i.core(t)
 
-    for part_i in scatter_i:
-        part_i.step(0)
+        @pl.when(i == 1)
+        def _():
+            for part_i in scatter_i:
+                part_i.step(0)
+
     weight_drain("qkv", wqkv_in, w_qkv)
     weight_drain("out", wout_in, w_out)
     n1_back.wait()
@@ -1416,7 +1424,7 @@
 
 
 def last_sums(*arrays):
-    steps = 8
+    steps = 4
     in_specs, out_specs, out_shape = [], [], []
     for i, array in enumerate(arrays):
         rows, cols = array.shape[-2:]

time: 302 us -> 298 us (0.987)
  Pallas kernels: 297 us -> 293 us
where the time goes in v4:
time: 298 us; the launch traced here: 297 us
  Pallas kernels  293 us (98%)
    pallas_call x1, Pallas kernels, per_device_fast(): pl.pallas_call(functools.partial(layer_kernel, plan, sem_at), out_shape=o...  285 us
    pallas_call x1, Pallas kernels, last_sums(): pl.pallas_call(last_sums_kernel, grid=(steps,), in_specs=in_specs, out_sp...  7.57 us

profile of v4, /device:TPU:0, one launch (start us, length us, event | category | flops | bytes accessed | tf_op | source)
XLA Modules:
  0.0 297.4 jit_solution(1978689204811997627)
XLA Ops:
  0.7 0.7 maximum_convert_fusion
  1.4 0.1 pad_select_fusion
  1.4 0.7 convert_element_type.10
  2.1 0.1 select_bitcast_fusion
  2.8 0.1 pad.6.clone
  2.9 0.7 maximum_maximum_fusion.refs_2_
  3.6 285.0 %shard_map.238 = (bf16[128,2048]{1,0:T(8,128)(2,1)}, f32[128,2048]{1,0:T(8,128)}, f32[8,384]{1,0:T(8,128)}, bf16[3,256,1536]{2,1,0:T(8,128)(2,1)}, bf16[3,512,25...) custom-call(bf16[128,2048]{1,0:T(8,128)(2,1)} %bitcast.21, ...), custom_call_target="tpu_custom_call" | custom-call | tf_op jit(solution)/shard_map/pallas_call | solution.py:1540
  288.6 0.0 copy-start
  288.6 7.6 %shard_map.239 = (bf16[128,2048]{1,0:T(8,128)(2,1)}, f32[128,2048]{1,0:T(8,128)}, f32[256,1536]{1,0:T(8,128)}, f32[512,256]{1,0:T(8,128)}, f32[256,1408]{1,0:T(8...) custom-call(bf16[128,2048]{1,0:T(8,128)(2,1)} %get-tuple-element.27.refs_0_, f32[128,2048]{1,0:T(8,128)} %get-tuple-element.28.refs_1_, ...), custom_call_target="tpu_custom_call" | custom-call | tf_op jit(solution)/shard_map/pallas_call | solution.py:1439
  296.1 0.0 copy-done
  296.2 0.1 constant_dynamic-slice_fusion
  296.2 0.5 slice_bitcast_fusion.1
  296.8 0.6 dynamic_slice.7
  (2 shorter events, 0.0 us)
Async XLA Ops:
  288.6 7.6 %copy-start = (f32[8,384]{1,0:T(8,128)S(1)}, f32[8,384]{1,0:T(8,128)}, u32[]{:S(2)}) copy-start(f32[8,384]{1,0:T(8,128)} %get-tuple-element.36) | copy-start | bytes 36868
